TPU v7x, 128 devices: a whole 4x4x4 slice. The times are simulated.
128 devices in a mesh: row: 16 (over y, z_lo, core), col: 8 (over z_hi, x).
Axes of the slice: x: 4, y: 4, z: 4 (z_hi: 2, z_lo: 2; z = z_hi * 2 + z_lo), core: 2. Of those that a mesh axis runs over, the one named last changes fastest.
Arguments:
- kv_cache: bfloat16 [256, 128, 2, 1536], P('row', 'col'), may hold values from -20 to 20
- fresh_qkv: bfloat16 [256, 128, 3, 1536], P('row', 'col'), may hold values from -20 to 20
- edit_list: int32 [4, 8], P(None, 'col'), may hold values from 0 to 16, as said below
Outputs:
- attended: bfloat16 [256, 128, 1536], P('row', 'col')
Inputs may be any that keep to these rules, and one draw needn't show every extreme that they name: `edit_list`: each column lists its distinct edited tile rows in increasing order, at least one, then 16 in the unused entries; some column lists 4 rows.
All inputs are finite; a program needn't handle non-finite values.
Results may differ from a plain program's by a relative error of at most 0.017.
Values may be sent and summed in bfloat16 or wider, within the bound.
No kernel may reach another device: no remote copies, remote signals or barrier semaphores. Data moves between devices by JAX's collectives and lax.ppermute only.
A program may use at most 256 MiB of HBM per device.

v0:
```python
import math

import jax
import jax.numpy as jnp
from jax import lax
from jax.sharding import PartitionSpec as P

HEADS = 12


def merged(part, axis, combine):
    gathered = jax.tree.map(lambda a: lax.all_gather(a, axis), part)

    def take(source):
        return jax.tree.map(lambda a: lax.dynamic_index_in_dim(a, source, 0, False), gathered)

    return lax.fori_loop(
        1, lax.axis_size(axis), lambda source, state: combine(state, take(source)), take(0)
    )


def join_partials(left_state, right_state):
    joint_max = jnp.maximum(left_state[0], right_state[0])
    left_weight = jnp.exp(left_state[0] - joint_max)
    right_weight = jnp.exp(right_state[0] - joint_max)
    joint_total = left_state[1] * left_weight + right_state[1] * right_weight
    joint_numer = (
        left_state[2] * left_weight[:, :, None] + right_state[2] * right_weight[:, :, None]
    )
    return (joint_max, joint_total, joint_numer)


def per_device(kv_cache, fresh_qkv, edit_list):
    tile_edge = kv_cache.shape[0]
    tile_width = kv_cache.shape[1]
    tile_toks = tile_edge * tile_width
    features = kv_cache.shape[3]
    head_count = HEADS
    head_size = features // head_count
    band_count = lax.axis_size("row")
    my_row = lax.axis_index("row")
    listed_rows = edit_list[:, 0]
    own_edited = jnp.any(listed_rows == my_row)
    own_kv = jnp.where(own_edited, fresh_qkv[:, :, 1:, :], kv_cache).reshape(tile_toks, 2, features)
    own_query = fresh_qkv[:, :, 0, :].reshape(tile_toks, features)
    safe_rows = jnp.minimum(listed_rows, band_count - 1)
    band_rows = lax.all_gather(own_query.reshape(1, tile_toks, features), "row", axis=0, tiled=True)
    picked = jnp.take(band_rows, safe_rows, axis=0)
    slot_count = picked.shape[0]
    query_count = slot_count * tile_toks
    queries = picked.reshape(query_count, head_count, head_size)
    score_scale = 1.0 / math.sqrt(head_size)
    initial = (
        jnp.full((head_count, query_count), -1e30, jnp.float32),
        jnp.zeros((head_count, query_count), jnp.float32),
        jnp.zeros((head_count, query_count, head_size), jnp.float32),
    )
    kv_piece = lax.all_gather(own_kv, "col", axis=0, tiled=True)
    piece_rows = kv_piece.shape[0]
    block_rows = math.gcd(piece_rows, 512)
    kv_blocks = kv_piece.reshape(piece_rows // block_rows, block_rows, 2, head_count, head_size)

    def absorb_block(carry_state, key_block):
        old_max, old_total, old_numer = carry_state
        scores = (
            jnp.einsum("qhd,khd->hqk", queries, key_block[:, 0], preferred_element_type=jnp.float32)
            * score_scale
        )
        new_max = jnp.maximum(old_max, jnp.max(scores, axis=2))
        shrink = jnp.exp(old_max - new_max)
        weights = jnp.exp(scores - new_max[:, :, None])
        new_total = old_total * shrink + jnp.sum(weights, axis=2)
        new_numer = old_numer * shrink[:, :, None] + jnp.einsum(
            "hqk,khd->hqd",
            weights.astype(jnp.bfloat16),
            key_block[:, 1],
            preferred_element_type=jnp.float32,
        )
        return ((new_max, new_total, new_numer), None)

    row_max, row_total, numerator = lax.scan(absorb_block, initial, kv_blocks)[0]
    row_max, row_total, numerator = merged((row_max, row_total, numerator), "row", join_partials)
    finished = (numerator / row_total[:, :, None]).astype(jnp.bfloat16)
    result = finished.reshape(head_count, slot_count, tile_toks, head_size)
    slot_found = jnp.argmax((listed_rows == my_row).astype(jnp.int32))
    own_result = lax.dynamic_index_in_dim(result, slot_found, 1, keepdims=False)
    own_result = own_result.transpose(1, 0, 2).reshape(tile_edge, tile_width, features)
    return jnp.where(own_edited, own_result, jnp.zeros_like(own_result))


def solution(mesh):
    placed = (P("row", "col", None, None), P("row", "col", None, None), P(None, "col"))
    return jax.shard_map(
        per_device, mesh=mesh, in_specs=placed, out_specs=P("row", "col", None), check_vma=False
    )
```

profile of v0, /device:TPU:1, one launch (start us, length us, event | category | flops | bytes accessed | tf_op | source)
XLA Modules:
  0.0 1078.4 jit_solution(1016663525037625746)
XLA Ops:
  14.4 148.0 %all-gather.9.cloned.1.call-done = bf16[2048,2,1536]{2,0,1:T(8,128)(2,1)} async-done(((bf16[256,2,1536]{2,0,1:T(8,128)(2,1)}), bf16[2048,2,1536]{2,0,1:T(8,128)(2,1)}) %all-gather.9.cloned.1.call-update) | async-done | bytes 12582928 | tf_op jit(solution)/shard_map/all_gather | solution.py:58
  162.4 23.4 %reshape.61 = bf16[4,512,2,12,128]{4,3,1,0,2:T(8,128)(2,1)} reshape(bf16[2048,2,1536]{2,0,1:T(8,128)(2,1)} %all-gather.9.cloned.1.call-done) | data formatting | bytes 25165824 | tf_op jit(solution)/shard_map/reshape | solution.py:61
  185.8 13.6 %copy.27 = bf16[4,512,2,12,128]{4,1,3,2,0:T(8,128)(2,1)} copy(bf16[4,512,2,12,128]{4,3,1,0,2:T(8,128)(2,1)} %reshape.61) | data formatting | bytes 25165824
  199.4 35.2 %all-gather.11.cloned.1.call-done = bf16[16,256,1536]{2,1,0:T(8,128)(2,1)} async-done(((bf16[1,256,1536]{2,1,0:T(8,128)(2,1)}), bf16[16,256,1536]{2,1,0:T(8,128)(2,1)}) %all-gather.11.cloned.1.call-update) | async-done | bytes 12582928 | tf_op jit(solution)/shard_map/all_gather | solution.py:47
  254.9 152.6 %while.35 = (s32[]{:T(128)}, f32[12,1024]{1,0:T(8,128)S(1)}, f32[12,1024]{1,0:T(8,128)S(1)}, f32[12,1024,128]{2,1,0:T(8,128)}, bf16[4,512,2,12,128]{4,1,3,2,0:T(...) while((s32[]{:T(128)}, f32[12,1024]{1,0:T(8,128)S(1)}, ...), condition=%wide.region_4.5_spmd.clone, body=%wide.region_1.0_spmd.clone.sunk | while | flops 3276337152 | bytes 114065544 | solution.py:81
  257.7 10.0 bitcast_reduce_fusion.2
  267.8 10.5 fusion.34
  278.3 13.1 %fusion.36 = f32[12,1024,128]{2,1,0:T(8,128)} fusion(f32[12,1024,128]{2,1,0:T(8,128)} %get-tuple-element.405, f32[12,1024]{1,0:T(8,128)S(1)} %get-tuple-element.393, pred[]{:T(512)S(6)} %compare.3, f32[12,512,1024]{2,1,0:T(8,128)} %get-tuple-element.391, f32[12,1024]{1,0:T(8,128)S(1)} %select_maximum_fusion.2, ...), kind=kOutput, calls=%fused_computation.18.clone.1 | convolution fusion | flops 1634205696 | bytes 39452672 | tf_op jit(solution)/shard_map/while/body/eval_jaxpr/hqk,khd->hqd/dot_general | solution.py:73
  294.3 10.0 bitcast_reduce_fusion.2
  304.4 10.5 fusion.34
  314.9 15.3 %fusion.36 = f32[12,1024,128]{2,1,0:T(8,128)} fusion(f32[12,1024,128]{2,1,0:T(8,128)} %get-tuple-element.405, f32[12,1024]{1,0:T(8,128)S(1)} %get-tuple-element.393, pred[]{:T(512)S(6)} %compare.3, f32[12,512,1024]{2,1,0:T(8,128)} %get-tuple-element.391, f32[12,1024]{1,0:T(8,128)S(1)} %select_maximum_fusion.2, ...), kind=kOutput, calls=%fused_computation.18.clone.1 | convolution fusion | flops 1634205696 | bytes 39452672 | tf_op jit(solution)/shard_map/while/body/eval_jaxpr/hqk,khd->hqd/dot_general | solution.py:73
  333.0 10.0 bitcast_reduce_fusion.2
  343.1 10.5 fusion.34
  353.6 15.3 %fusion.36 = f32[12,1024,128]{2,1,0:T(8,128)} fusion(f32[12,1024,128]{2,1,0:T(8,128)} %get-tuple-element.405, f32[12,1024]{1,0:T(8,128)S(1)} %get-tuple-element.393, pred[]{:T(512)S(6)} %compare.3, f32[12,512,1024]{2,1,0:T(8,128)} %get-tuple-element.391, f32[12,1024]{1,0:T(8,128)S(1)} %select_maximum_fusion.2, ...), kind=kOutput, calls=%fused_computation.18.clone.1 | convolution fusion | flops 1634205696 | bytes 39452672 | tf_op jit(solution)/shard_map/while/body/eval_jaxpr/hqk,khd->hqd/dot_general | solution.py:73
  371.7 10.0 bitcast_reduce_fusion.2
  381.8 10.5 fusion.34
  392.3 15.3 %fusion.36 = f32[12,1024,128]{2,1,0:T(8,128)} fusion(f32[12,1024,128]{2,1,0:T(8,128)} %get-tuple-element.405, f32[12,1024]{1,0:T(8,128)S(1)} %get-tuple-element.393, pred[]{:T(512)S(6)} %compare.3, f32[12,512,1024]{2,1,0:T(8,128)} %get-tuple-element.391, f32[12,1024]{1,0:T(8,128)S(1)} %select_maximum_fusion.2, ...), kind=kOutput, calls=%fused_computation.18.clone.1 | convolution fusion | flops 1634205696 | bytes 39452672 | tf_op jit(solution)/shard_map/while/body/eval_jaxpr/hqk,khd->hqd/dot_general | solution.py:73
  411.0 25.2 %all-gather.3 = f32[16,12,1024]{2,1,0:T(8,128)S(1)} all-gather(f32[1,12,1024]{2,1,0:T(8,128)S(1)} %bitcast.82), channel_id=2, replica_groups=mesh['row'=16,'col'=8] {'row'}, dimensions={0}, use_global_device_ids=true | all-gather | bytes 835584 | tf_op jit(solution)/shard_map/all_gather | solution.py:12
  436.3 25.2 %all-gather.4 = f32[16,12,1024]{2,1,0:T(8,128)S(1)} all-gather(f32[1,12,1024]{2,1,0:T(8,128)S(1)} %bitcast.86), channel_id=3, replica_groups=mesh['row'=16,'col'=8] {'row'}, dimensions={0}, use_global_device_ids=true | all-gather | bytes 835584 | tf_op jit(solution)/shard_map/all_gather | solution.py:12
  461.5 450.7 %all-gather.13.cloned.1.call-done = f32[192,1024,128]{2,1,0:T(8,128)} async-done(((f32[12,1024,128]{2,1,0:T(8,128)}), f32[192,1024,128]{2,1,0:T(8,128)}) %all-gather.13.cloned.1.call-update) | async-done | bytes 100663312 | tf_op jit(solution)/shard_map/all_gather | solution.py:12
  917.9 146.9 %while.34 = (s32[]{:T(128)}, f32[12,1024]{1,0:T(8,128)S(1)}, f32[12,1024]{1,0:T(8,128)S(1)}, f32[12,1024,128]{2,1,0:T(8,128)}, f32[16,12,1024]{2,1,0:T(8,128)S(1...) while((s32[]{:T(128)}, f32[12,1024]{1,0:T(8,128)S(1)}, ...), condition=%wide.region_6.7_spmd, body=%wide.region_5.6_spmd.sunk | while | flops 4792325 | bytes 19366032 | solution.py:17
  918.0 9.7 fusion.31
  927.8 9.7 fusion.31
  937.6 9.7 fusion.31
  947.4 9.7 fusion.31
  957.2 9.7 fusion.31
  967.0 9.7 fusion.31
  976.8 9.7 fusion.31
  986.6 9.7 fusion.31
  996.4 9.7 fusion.31
  1006.2 9.7 fusion.31
  1016.0 9.7 fusion.31
  (76 shorter events, 93.5 us)
Async XLA Ops:
  6.5 7.8 copy-start.1
  6.5 155.9 %all-gather.9.cloned.1.call-start = ((), (), s32[]{:S(2)}) async-start(), calls=%async_computation | async-start | bytes 14155776 | tf_op jit(solution)/shard_map/all_gather | solution.py:58
  12.0 222.6 %all-gather.11.cloned.1.call-start = ((), (), s32[]{:S(2)}) async-start(), calls=%async_computation.1 | async-start | bytes 13369344 | tf_op jit(solution)/shard_map/all_gather | solution.py:47
  14.2 898.0 %all-gather.13.cloned.1.call-start = ((), (), s32[]{:S(2)}) async-start(), calls=%async_computation.2 | async-start | bytes 106954752 | tf_op jit(solution)/shard_map/all_gather | solution.py:12
  254.9 2.8 copy-start
  291.5 2.8 copy-start
  330.2 2.8 copy-start
  368.9 2.8 copy-start
  407.6 0.7 copy-start.2
Sparse Core Ops, SparseCore 0:
  12.2 150.1 all-gather.8
  164.1 70.4 all-gather.10
  407.7 504.4 all-gather.12
where the time goes:
time: 1080 us
  waiting for transfers between devices  634 us (59%)
  other arithmetic  203 us (19%)
  matrix products  99.1 us (9%)
  local copies, waits for them, and re-layouts  76.7 us (7%)
  blocking collectives  50.4 us (5%)
  between operations  15.3 us (1%)
    all_gather x1, waiting for transfers between devices, merged(): gathered = jax.tree.map(lambda a: lax.all_gather(a, axis), part)  451 us
    all_gather x1, waiting for transfers between devices, per_device(): kv_piece = lax.all_gather(own_kv, 'col', axis=0, tiled=True)  148 us
    add x15, other arithmetic, join_partials(): left_state[2] * left_weight[:, :, None]  146 us
    dot_general x4, matrix products, absorb_block(): jnp.einsum('hqk,khd->hqd', weights.astype(jnp.bfloat16), key_block[:, 1],...  59 us
    all_gather x2, blocking collectives, merged(): gathered = jax.tree.map(lambda a: lax.all_gather(a, axis), part)  50.4 us
    reduce_sum x4, other arithmetic, absorb_block(): new_total = old_total * shrink + jnp.sum(weights, axis=2)  41.8 us
    dot_general x4, matrix products, absorb_block(): jnp.einsum('qhd,khd->hqk', queries, key_block[:, 0], preferred_element_ty...  40.2 us
    all_gather x1, waiting for transfers between devices, per_device(): lax.all_gather(own_query.reshape(1, tile_toks, features), 'row', axis=0,...  35.2 us
  transfers between devices with their start and end apart: 3, of which 3 were waited for; matrix products, arithmetic and copies ran while one was open for 4% of the time, Pallas kernels for 0%

commit v1 on v0

v1 whole, which is shorter than its diff:
```python
import math

import jax
import jax.numpy as jnp
from jax import lax
from jax.experimental import pallas as pl
from jax.experimental.pallas import tpu as pltpu
from jax.sharding import Mesh, PartitionSpec as P

DEPTH = 128
SLOTS = 4
TOKS = 256
HALF = 128
QUART = 64
KV_ROWS = 4 * HALF
Q_ROWS = HALF + QUART
MSG_ROWS = KV_ROWS + Q_ROWS
SLOT_ROWS = Q_ROWS + 16
GROUP = 4
KEY_BLOCK = 512
MIB = 1024 * 1024


def vmem():
    return pl.BlockSpec(memory_space=pltpu.VMEM)


def smem():
    return pl.BlockSpec(memory_space=pltpu.SMEM)


def pack_kernel(q_ref, k_ref, v_ref, out_ref):
    for chip in range(2):
        full = slice(0, DEPTH) if chip == 0 else slice(2 * DEPTH, 3 * DEPTH)
        shared = slice(DEPTH, 2 * DEPTH)
        for core in range(2):
            dest = chip * 2 + core
            toks = slice(core * HALF, (core + 1) * HALF)
            quart = slice(core * HALF + chip * QUART, core * HALF + (chip + 1) * QUART)
            out_ref[dest, 0:HALF, :] = k_ref[toks, full]
            out_ref[dest, HALF : 2 * HALF, :] = v_ref[toks, full]
            out_ref[dest, 2 * HALF : 3 * HALF, :] = k_ref[toks, shared]
            out_ref[dest, 3 * HALF : 4 * HALF, :] = v_ref[toks, shared]
            out_ref[dest, KV_ROWS : KV_ROWS + HALF, :] = q_ref[toks, full]
            out_ref[dest, KV_ROWS + HALF : MSG_ROWS, :] = q_ref[quart, shared]


def pack(query, keys, values):
    spec = pl.BlockSpec((TOKS, 3 * DEPTH), lambda p: (0, p))
    return pl.pallas_call(
        pack_kernel,
        grid=(4,),
        in_specs=[spec] * 3,
        out_specs=pl.BlockSpec((4, MSG_ROWS, DEPTH), lambda p: (p, 0, 0)),
        out_shape=jax.ShapeDtypeStruct((16, MSG_ROWS, DEPTH), jnp.bfloat16),
    )(query, keys, values)


def attend_rows(queries, k_refs, kv_refs, head, vext):
    fold = math.log2(math.e) / math.sqrt(DEPTH)
    row_max = None
    acc = None
    blocks = 2048 // KEY_BLOCK
    tiles = KEY_BLOCK // HALF
    first = 2 * HALF * head
    for part in range(2):
        for block in range(blocks):
            rows = slice(block * tiles, (block + 1) * tiles)
            keys = kv_refs[part][rows, first : first + HALF, :].reshape(KEY_BLOCK, DEPTH)
            scores = (
                lax.dot_general(
                    queries, keys, (((1,), (1,)), ((), ())), preferred_element_type=jnp.float32
                )
                * fold
            )
            block_max = jnp.max(scores, axis=1, keepdims=True)
            new_max = block_max if row_max is None else jnp.maximum(row_max, block_max)
            weights = jnp.exp2(scores - new_max).astype(jnp.bfloat16)
            start = part * 2048 + block * KEY_BLOCK
            term = jnp.dot(
                weights,
                vext[head, start : start + KEY_BLOCK, :],
                preferred_element_type=jnp.float32,
            )
            if row_max is None:
                acc = term
            else:
                acc = acc * jnp.exp2(row_max - new_max) + term
            row_max = new_max
    total = acc[:, DEPTH:]
    out = (acc[:, :DEPTH] / total).astype(jnp.bfloat16)
    return out, jnp.log2(total) + row_max


def attend_kernel(valid_ref, q_ref, own_ref, other_ref, out_ref, vext, table):
    slots = q_ref.shape[0]
    for head in range(2):
        first = 2 * HALF * head + HALF
        vext[head, 0:2048, 0:DEPTH] = own_ref[:, first : first + HALF, :].reshape(2048, DEPTH)
        vext[head, 2048:4096, 0:DEPTH] = other_ref[:, first : first + HALF, :].reshape(2048, DEPTH)
        vext[head, :, DEPTH:] = jnp.ones((4096, DEPTH), jnp.bfloat16)

    def note(slot, count):
        is_valid = valid_ref[slot]

        @pl.when(is_valid == 1)
        def _():
            table[count] = slot

        return count + is_valid

    count = lax.fori_loop(0, slots, note, jnp.int32(0))
    for extra in range(GROUP):
        table[count + extra] = table[0]

    kv_refs = (own_ref, other_ref)

    def body(group, carry):
        picks = [table[group * GROUP + i] for i in range(GROUP)]
        full = jnp.concatenate([q_ref[pick, 0:HALF, :] for pick in picks], axis=0)
        out_full, lse_full = attend_rows(full, None, kv_refs, 0, vext)
        shared = jnp.concatenate([q_ref[pick, HALF:Q_ROWS, :] for pick in picks], axis=0)
        out_shared, lse_shared = attend_rows(shared, None, kv_refs, 1, vext)
        row_ids = lax.broadcasted_iota(jnp.int32, (16, DEPTH), 0)
        for i, pick in enumerate(picks):
            out_ref[pick, 0:HALF, :] = out_full[i * HALF : (i + 1) * HALF]
            out_ref[pick, HALF:Q_ROWS, :] = out_shared[i * QUART : (i + 1) * QUART]
            lse_one = lse_shared[i * QUART : (i + 1) * QUART]
            pair = (
                jnp.transpose(lse_full[i * HALF : (i + 1) * HALF]),
                jnp.transpose(jnp.concatenate([lse_one, lse_one], axis=0)),
            )
            stats = jnp.zeros((16, DEPTH), jnp.float32)
            for j, lanes in enumerate(pair):
                rest = lanes[0:16]
                for term in range(3):
                    piece = rest.astype(jnp.bfloat16).astype(jnp.float32)
                    rest = rest - piece
                    stats = jnp.where(row_ids == 3 * j + term, piece, stats)
            out_ref[pick, Q_ROWS:SLOT_ROWS, :] = stats.astype(jnp.bfloat16)
        return carry

    lax.fori_loop(0, pl.cdiv(count, GROUP), body, 0)


def attend(valid, queries, own, other):
    slots = queries.shape[0]
    return pl.pallas_call(
        attend_kernel,
        in_specs=[smem(), vmem(), vmem(), vmem()],
        out_specs=vmem(),
        out_shape=jax.ShapeDtypeStruct((slots, SLOT_ROWS, DEPTH), jnp.bfloat16),
        scratch_shapes=[
            pltpu.VMEM((2, 4096, 2 * DEPTH), jnp.bfloat16),
            pltpu.SMEM((slots + GROUP,), jnp.int32),
        ],
        compiler_params=pltpu.CompilerParams(vmem_limit_bytes=48 * MIB),
    )(valid, queries, own, other)


def combine_kernel(rows_ref, part_ref, out_ref):
    out_ref[...] = jnp.zeros_like(out_ref)
    band_count = out_ref.shape[0]
    sources = part_ref.shape[0]
    for slot in range(SLOTS):
        row = rows_ref[slot]

        @pl.when(row < band_count)
        def _():
            stats = [
                part_ref[i, slot, Q_ROWS:SLOT_ROWS, :].astype(jnp.float32) for i in range(sources)
            ]
            for j, (first, size) in enumerate(((0, HALF), (HALF, QUART))):
                lses = [s[3 * j : 3 * j + 1] + s[3 * j + 1 : 3 * j + 2] + s[3 * j + 2 : 3 * j + 3] for s in stats]
                top = lses[0]
                for lse in lses[1:]:
                    top = jnp.maximum(top, lse)
                shares = [jnp.exp2(lse - top) for lse in lses]
                whole = shares[0]
                for share in shares[1:]:
                    whole = whole + share
                total = jnp.zeros((size, DEPTH), jnp.float32)
                for i in range(sources):
                    share = jnp.broadcast_to(shares[i] / whole, (DEPTH, DEPTH))
                    total = total + jnp.transpose(share)[0:size] * part_ref[
                        i, slot, first : first + size, :
                    ].astype(jnp.float32)
                out_ref[row, first : first + size, :] = total.astype(jnp.bfloat16)


def combine(listed_rows, partials, band_count):
    return pl.pallas_call(
        combine_kernel,
        in_specs=[smem(), vmem()],
        out_specs=vmem(),
        out_shape=jax.ShapeDtypeStruct((band_count, Q_ROWS, DEPTH), jnp.bfloat16),
        compiler_params=pltpu.CompilerParams(vmem_limit_bytes=24 * MIB),
    )(listed_rows, partials)


def unpack_kernel(in_ref, out_ref):
    for chip in range(2):
        full = slice(0, DEPTH) if chip == 0 else slice(2 * DEPTH, 3 * DEPTH)
        for core in range(2):
            source = chip * 2 + core
            first = core * HALF + chip * QUART
            out_ref[core * HALF : (core + 1) * HALF, full] = in_ref[source, 0:HALF, :]
            out_ref[first : first + QUART, DEPTH : 2 * DEPTH] = in_ref[source, HALF:Q_ROWS, :]


def unpack(received, features):
    return pl.pallas_call(
        unpack_kernel,
        grid=(4,),
        in_specs=[pl.BlockSpec((4, Q_ROWS, DEPTH), lambda p: (p, 0, 0))],
        out_specs=pl.BlockSpec((TOKS, 3 * DEPTH), lambda p: (0, p)),
        out_shape=jax.ShapeDtypeStruct((TOKS, features), jnp.bfloat16),
    )(received)


def per_device(kv_cache, fresh_qkv, edit_list):
    tile_edge, tile_width, _, features = kv_cache.shape
    row_axes = ("chip", "core")
    band_count = lax.axis_size(row_axes)
    col_count = lax.axis_size("col")
    my_row = lax.axis_index(row_axes)
    listed_rows = edit_list[:, 0]
    own_edited = jnp.any(listed_rows == my_row)
    keys = jnp.where(own_edited, fresh_qkv[:, :, 1, :], kv_cache[:, :, 0, :])
    values = jnp.where(own_edited, fresh_qkv[:, :, 2, :], kv_cache[:, :, 1, :])
    query = fresh_qkv[:, :, 0, :]
    flat = (TOKS, features)
    message = pack(query.reshape(flat), keys.reshape(flat), values.reshape(flat))
    received = lax.all_to_all(message, row_axes, 0, 0, tiled=True)
    other = lax.ppermute(received[:, :KV_ROWS], "core", [(0, 1), (1, 0)])

    safe_rows = jnp.minimum(listed_rows, band_count - 1)
    picked = jnp.stack(
        [
            lax.dynamic_slice(received, (safe_rows[s], KV_ROWS, 0), (1, Q_ROWS, DEPTH))[0]
            for s in range(SLOTS)
        ]
    )
    flags = (listed_rows < band_count).astype(jnp.bfloat16)
    heads = jnp.broadcast_to(flags[:, None, None], (SLOTS, 16, DEPTH))
    mine = jnp.concatenate([picked, heads], axis=1)
    spread = jnp.broadcast_to(mine[None], (col_count,) + mine.shape)
    queries = lax.all_to_all(spread, "col", 0, 0, tiled=True)
    queries = queries.reshape(col_count * SLOTS, SLOT_ROWS, DEPTH)
    valid = queries[:, Q_ROWS, 0].astype(jnp.int32)

    partials = attend(valid, queries, received, other)
    partials = partials.reshape(col_count, SLOTS, SLOT_ROWS, DEPTH)
    partials = lax.all_to_all(partials, "col", 0, 0, tiled=True)
    finished = combine(listed_rows, partials, band_count)
    finished = lax.all_to_all(finished, row_axes, 0, 0, tiled=True)
    return unpack(finished, features).reshape(tile_edge, tile_width, features)


def solution(mesh):
    rows, cols = mesh.devices.shape
    fine = Mesh(mesh.devices.reshape(rows // 2, 2, cols), ("chip", "core", "col"))
    split = ("chip", "core")
    placed = (P(split, "col", None, None), P(split, "col", None, None), P(None, "col"))
    return jax.shard_map(
        per_device, mesh=fine, in_specs=placed, out_specs=P(split, "col", None), check_vma=False
    )
```

time: 1080 us -> 170 us (0.16)
  waiting for transfers between devices: 634 us -> 0.01 us
  other arithmetic: 203 us -> 5.08 us
  matrix products: 99.1 us -> 0 us
  local copies, waits for them, and re-layouts: 76.7 us -> 8.97 us
  blocking collectives: 50.4 us -> 118 us
  Pallas kernels: 0 us -> 29.6 us
    all_gather x3 -> x0, waiting for transfers between devices: 634 us -> none  [the longest x1 451 us: merged(): gathered = jax.tree.map(lambda a: lax.all_gather(a, axis), part)]
    add x34 -> x0, other arithmetic: 147 us -> none  [the longest x15 146 us: join_partials(): left_state[2] * left_weight[:, :, None]]
    all_to_all x0 -> x4, blocking collectives: none -> 118 us  [the longest x1 42.8 us: per_device(): received = lax.all_to_all(message, row_axes, 0, 0, tiled=True)]
    dot_general x8 -> x0, matrix products: 99.1 us -> none  [the longest x4 59 us: absorb_block(): jnp.einsum('hqk,khd->hqd', weights.astype(jnp.bfloat16), key_block[:, 1],...]
    all_gather x2 -> x0, blocking collectives: 50.4 us -> none  [merged(): gathered = jax.tree.map(lambda a: lax.all_gather(a, axis), part)]
    reduce_sum x4 -> x0, other arithmetic: 41.8 us -> none  [absorb_block(): new_total = old_total * shrink + jnp.sum(weights, axis=2)]
    pallas_call x0 -> x4, Pallas kernels: none -> 29.6 us  [the longest x1 20.8 us: attend(): pl.pallas_call(attend_kernel, in_specs=[smem(), vmem(), vmem(), vmem()],...]
    reshape x1 -> x0, local copies, waits for them, and re-layouts: 23.4 us -> none  [per_device(): kv_piece.reshape(piece_rows // block_rows, block_rows, 2, head_count, hea...]
  transfers between devices with their start and end apart: 3 -> 1, of which waited for: 3 -> 0; matrix products, arithmetic and copies ran while one was open for 4% -> 2% of each run, Pallas kernels for 0% -> 0%
where the time goes in v1:
time: 170 us; the launch traced here: 169 us
  blocking collectives  118 us (69%)
  Pallas kernels  29.6 us (17%)
  local copies, waits for them, and re-layouts  8.97 us (5%)
  between operations  7.4 us (4%)
  other arithmetic  5.08 us (3%)
    all_to_all x1, blocking collectives, per_device(): received = lax.all_to_all(message, row_axes, 0, 0, tiled=True)  42.8 us
    all_to_all x1, blocking collectives, per_device(): queries = lax.all_to_all(spread, 'col', 0, 0, tiled=True)  30.9 us
    all_to_all x1, blocking collectives, per_device(): partials = lax.all_to_all(partials, 'col', 0, 0, tiled=True)  25.1 us
    pallas_call x1, Pallas kernels, attend(): pl.pallas_call(attend_kernel, in_specs=[smem(), vmem(), vmem(), vmem()],...  20.8 us
    all_to_all x1, blocking collectives, per_device(): finished = lax.all_to_all(finished, row_axes, 0, 0, tiled=True)  18.6 us
    slice x1, local copies, waits for them, and re-layouts, per_device(): values = jnp.where(own_edited, fresh_qkv[:, :, 2, :], kv_cache[:, :, 1, :])  4.79 us
    pallas_call x1, Pallas kernels, pack(): pl.pallas_call(pack_kernel, grid=(4,), in_specs=[spec] * 3, out_specs=pl....  4.19 us
    select_n x1, other arithmetic, per_device(): values = jnp.where(own_edited, fresh_qkv[:, :, 2, :], kv_cache[:, :, 1, :])  3.7 us
  transfers between devices with their start and end apart: 1, of which 0 were waited for; matrix products, arithmetic and copies ran while one was open for 2% of the time, Pallas kernels for 0%

profile of v1, /device:TPU:1, one launch (start us, length us, event | category | flops | bytes accessed | tf_op | source)
XLA Modules:
  0.0 169.0 jit_solution(1337755841013683129)
XLA Ops:
  0.0 0.0 copy-start
  0.0 4.8 %fusion.1 = (bf16[16,16,1,1536]{3,2,1,0:T(2,128)(2,1)S(1)}, bf16[16,16,1,1536]{3,2,1,0:T(2,128)(2,1)S(1)}) fusion(bf16[16,16,2,1536]{3,2,1,0:T(2,128)(2,1)} %param.3), kind=kLoop, calls=%fused_computation.12 | loop fusion | bytes 3145728 | tf_op jit(solution)/shard_map/slice | solution.py:230
  4.8 0.0 copy-done
  4.8 0.7 compare_reduce_fusion
  5.5 3.7 %copy_select_fusion = (bf16[16,16,1,1536]{3,1,2,0:T(8,128)(2,1)}, bf16[16,16,1,1536]{3,1,2,0:T(8,128)(2,1)}, bf16[16,16,1,1536]{3,1,2,0:T(8,128)(2,1)}) fusion(bf16[16,16,1,1536]{3,2,1,0:T(2,128)(2,1)S(1)} %get-tuple-element.12, bf16[16,16,3,1536]{3,1,2,0:T(8,128)(2,1)} %param.4, pred[]{:T(512)} %get-tuple-element.18, ...), kind=kLoop, calls=%fused_computation | loop fusion | flops 786432 | bytes 6291457 | tf_op jit(solution)/shard_map/jit(_where)/select_n | solution.py:230
  9.2 4.2 %shard_map.37 = bf16[16,704,128]{2,1,0:T(8,128)(2,1)} custom-call(bf16[256,1536]{1,0:T(8,128)(2,1)} %bitcast.19, bf16[256,1536]{1,0:T(8,128)(2,1)} %bitcast.20, bf16[256,1536]{1,0:T(8,128)(2,1)} %bitcast.18), custom_call_target="tpu_custom_call" | custom-call | tf_op jit(solution)/shard_map/pallas_call | solution.py:50
  13.4 42.8 %all_to_all.20.own_ref = bf16[16,704,128]{2,1,0:T(8,128)(2,1)S(1)} all-to-all(bf16[16,704,128]{2,1,0:T(8,128)(2,1)} %shard_map.37), channel_id=1, replica_groups=mesh['chip'=8,'core'=2,'col'=8] {'chip','core'}, dimensions={0} | all-to-all | bytes 5767168 | tf_op jit(solution)/shard_map/all_to_all | solution.py:234
  56.2 0.0 copy-start.1
  56.2 1.6 slice.45
  57.8 0.7 copy-done.1
  58.5 0.4 collective-permute-start
  58.9 0.7 fusion.2
  66.9 0.9 constant_dynamic-slice_fusion.3
  67.9 0.1 broadcast_in_dim.4
  68.0 0.2 broadcast_in_dim.5
  68.2 30.9 %all_to_all.21 = bf16[8,4,208,128]{3,2,1,0:T(8,128)(2,1)S(1)} all-to-all(bf16[8,4,208,128]{3,2,1,0:T(8,128)(2,1)S(1)} %broadcast_in_dim.5), channel_id=1, replica_groups=mesh['chip'=8,'core'=2,'col'=8] {'col'}, dimensions={0} | all-to-all | bytes 3407872 | tf_op jit(solution)/shard_map/all_to_all | solution.py:248
  99.1 0.7 fusion.valid_ref
  99.7 0.0 collective-permute-done.other_ref
  99.8 20.8 %shard_map.38 = bf16[32,208,128]{2,1,0:T(8,128)(2,1)S(1)} custom-call(s32[32]{0:T(128)S(1)} %fusion.valid_ref, bf16[32,208,128]{2,1,0:T(8,128)(2,1)S(1)} %bitcast.15, bf16[16,704,128]{2,1,0:T(8,128)(2,1)} %copy-done.1, bf16[16,512,128]{2,1,0:T(8,128)(2,1)S(1)} %collective-permute-done.other_ref), custom_call_target="tpu_custom_call" | custom-call | tf_op jit(solution)/shard_map/pallas_call | solution.py:148
  120.5 25.1 %all_to_all.22.part_ref = bf16[8,4,208,128]{3,2,1,0:T(8,128)(2,1)S(1)} all-to-all(bf16[8,4,208,128]{3,2,1,0:T(8,128)(2,1)S(1)} %bitcast.16), channel_id=1, replica_groups=mesh['chip'=8,'core'=2,'col'=8] {'col'}, dimensions={0} | all-to-all | bytes 3407872 | tf_op jit(solution)/shard_map/all_to_all | solution.py:254
  145.7 1.4 shard_map.39
  147.0 18.6 %all_to_all.23.in_ref = bf16[16,192,128]{2,1,0:T(8,128)(2,1)} all-to-all(bf16[16,192,128]{2,1,0:T(8,128)(2,1)S(1)} %shard_map.39), channel_id=1, replica_groups=mesh['chip'=8,'core'=2,'col'=8] {'chip','core'}, dimensions={0} | all-to-all | bytes 1572864 | tf_op jit(solution)/shard_map/all_to_all | solution.py:256
  165.7 3.3 %shard_map.40 = bf16[256,1536]{1,0:T(8,128)(2,1)} custom-call(bf16[16,192,128]{2,1,0:T(8,128)(2,1)} %all_to_all.23.in_ref), custom_call_target="tpu_custom_call" | custom-call | tf_op jit(solution)/shard_map/pallas_call | solution.py:212
  (2 shorter events, 0.0 us)
Async XLA Ops:
  0.0 4.8 %copy-start = (s32[4,1]{0,1:T(1,128)S(1)}, s32[4,1]{0,1:T(1,128)}, u32[]{:S(2)}) copy-start(s32[4,1]{0,1:T(1,128)} %param.5) | copy-start | bytes 52
  56.2 2.3 %copy-start.1 = (bf16[16,704,128]{2,1,0:T(8,128)(2,1)}, bf16[16,704,128]{2,1,0:T(8,128)(2,1)S(1)}, u32[]{:S(2)}) copy-start(bf16[16,704,128]{2,1,0:T(8,128)(2,1)S(1)} %all_to_all.20.own_ref) | copy-start | bytes 8650756
  58.5 41.2 %collective-permute-start = (bf16[16,512,128]{2,1,0:T(8,128)(2,1)}, bf16[16,512,128]{2,1,0:T(8,128)(2,1)S(1)}, u32[]{:S(2)}, u32[]{:S(2)}) collective-permute-start(bf16[16,512,128]{2,1,0:T(8,128)(2,1)} %slice.45), channel_id=1, source_target_pairs={{0,8},{8,0},{1,9},{9,1},{2,10},{10,2},{3,11},{11,3},{4,12},{12,4},... | collective-permute-start | bytes 6291464 | tf_op jit(solution)/shard_map/ppermute | solution.py:235

commit v2 on v1

v2 whole, which is shorter than its diff:
```python
import functools
import math

import jax
import jax.numpy as jnp
from jax import lax
from jax.experimental import pallas as pl
from jax.experimental.pallas import tpu as pltpu
from jax.sharding import Mesh, PartitionSpec as P

DEPTH = 128
SLOTS = 4
TOKS = 256
HALF = 128
QUART = 64
KV_ROWS = 4 * HALF
Q_ROWS = HALF + QUART
MSG_ROWS = KV_ROWS + Q_ROWS
SLOT_ROWS = Q_ROWS + 16
GROUP = 4
KEY_BLOCK = 512
MIB = 1024 * 1024


def vmem():
    return pl.BlockSpec(memory_space=pltpu.VMEM)


def smem():
    return pl.BlockSpec(memory_space=pltpu.SMEM)


def cost(flops, moved):
    return pl.CostEstimate(flops=flops, bytes_accessed=moved, transcendentals=0)


def fresh_spec(part):
    return pl.BlockSpec((16, 1, 16, 3 * DEPTH), lambda p: (0, part, 0, p))


def pack_kernel(row_axes, rows_ref, cache_ref, query_ref, keys_ref, values_ref, out_ref):
    my_row = lax.axis_index(row_axes)
    edited = rows_ref[0] == my_row
    for slot in range(1, SLOTS):
        edited = jnp.logical_or(edited, rows_ref[slot] == my_row)

    def place(core, head, keys, values):
        for chip in ((0,), (0, 1), (1,))[head]:
            first = 2 * HALF if head == 1 else 0
            out_ref[chip * 2 + core, first : first + HALF, :] = keys
            out_ref[chip * 2 + core, first + HALF : first + 2 * HALF, :] = values

    for chip in range(2):
        full = slice(0, DEPTH) if chip == 0 else slice(2 * DEPTH, 3 * DEPTH)
        for core in range(2):
            dest = chip * 2 + core
            rows = slice(core * 8, core * 8 + 8)
            quart = slice(core * 8 + chip * 4, core * 8 + chip * 4 + 4)
            out_ref[dest, KV_ROWS : KV_ROWS + HALF, :] = query_ref[rows, 0, :, full].reshape(
                HALF, DEPTH
            )
            out_ref[dest, KV_ROWS + HALF : MSG_ROWS, :] = query_ref[
                quart, 0, :, DEPTH : 2 * DEPTH
            ].reshape(QUART, DEPTH)

    @pl.when(edited)
    def _():
        for core in range(2):
            rows = slice(core * 8, core * 8 + 8)
            for head in range(3):
                cols = slice(head * DEPTH, (head + 1) * DEPTH)
                place(
                    core,
                    head,
                    keys_ref[rows, 0, :, cols].reshape(HALF, DEPTH),
                    values_ref[rows, 0, :, cols].reshape(HALF, DEPTH),
                )

    @pl.when(jnp.logical_not(edited))
    def _():
        place_id = lax.broadcasted_iota(jnp.int32, (TOKS, TOKS), 0)
        source_id = lax.broadcasted_iota(jnp.int32, (TOKS, TOKS), 1)
        wanted = jnp.where(place_id < HALF, 2 * place_id, 2 * place_id - (TOKS - 1))
        sorter = (source_id == wanted).astype(jnp.float32).astype(jnp.bfloat16)
        for core in range(2):
            pairs = cache_ref[core * 8 : core * 8 + 8].reshape(TOKS, 3 * DEPTH)
            apart = jnp.dot(sorter, pairs, preferred_element_type=jnp.float32)
            apart = apart.astype(jnp.bfloat16)
            for head in range(3):
                cols = slice(head * DEPTH, (head + 1) * DEPTH)
                place(core, head, apart[0:HALF, cols], apart[HALF:TOKS, cols])


def pack(row_axes, listed_rows, cache, fresh):
    return pl.pallas_call(
        functools.partial(pack_kernel, row_axes),
        grid=(4,),
        in_specs=[
            smem(),
            pl.BlockSpec((16, 16, 2, 3 * DEPTH), lambda p: (0, 0, 0, p)),
            fresh_spec(0),
            fresh_spec(1),
            fresh_spec(2),
        ],
        out_specs=pl.BlockSpec((4, MSG_ROWS, DEPTH), lambda p: (p, 0, 0)),
        out_shape=jax.ShapeDtypeStruct((16, MSG_ROWS, DEPTH), jnp.bfloat16),
        cost_estimate=cost(0, 9 * 786432),
        compiler_params=pltpu.CompilerParams(vmem_limit_bytes=56 * MIB),
    )(listed_rows, cache, fresh, fresh, fresh)


def pick_kernel(rows_ref, got_ref, out_ref):
    bands = got_ref.shape[0]
    for slot in range(SLOTS):
        row = rows_ref[slot]
        rows = got_ref[jnp.minimum(row, bands - 1), KV_ROWS:MSG_ROWS, :]
        flag = jnp.where(row < bands, 1.0, 0.0)
        flags = jnp.full((SLOT_ROWS - Q_ROWS, DEPTH), flag, jnp.float32).astype(jnp.bfloat16)
        for dest in range(out_ref.shape[0]):
            out_ref[dest, slot, 0:Q_ROWS, :] = rows
            out_ref[dest, slot, Q_ROWS:SLOT_ROWS, :] = flags


def pick(listed_rows, received, copies):
    return pl.pallas_call(
        pick_kernel,
        in_specs=[smem(), vmem()],
        out_specs=vmem(),
        out_shape=jax.ShapeDtypeStruct((copies, SLOTS, SLOT_ROWS, DEPTH), jnp.bfloat16),
        cost_estimate=cost(0, 2 * 1703936),
        compiler_params=pltpu.CompilerParams(vmem_limit_bytes=16 * MIB),
    )(listed_rows, received)


def attend_rows(queries, kv_refs, head):
    fold = math.log2(math.e) / math.sqrt(DEPTH)
    row_max = total = acc = None
    tiles = KEY_BLOCK // HALF
    first = 2 * HALF * head
    for kv_ref in kv_refs:
        for block in range(kv_ref.shape[0] // tiles):
            rows = slice(block * tiles, (block + 1) * tiles)
            keys = kv_ref[rows, first : first + HALF, :].reshape(KEY_BLOCK, DEPTH)
            values = kv_ref[rows, first + HALF : first + 2 * HALF, :].reshape(KEY_BLOCK, DEPTH)
            scores = lax.dot_general(
                queries, keys, (((1,), (1,)), ((), ())), preferred_element_type=jnp.float32
            )
            scores = scores * fold
            block_max = jnp.max(scores, axis=1, keepdims=True)
            new_max = block_max if row_max is None else jnp.maximum(row_max, block_max)
            weights = jnp.exp2(scores - new_max)
            block_total = jnp.sum(weights, axis=1, keepdims=True)
            term = jnp.dot(
                weights.astype(jnp.bfloat16), values, preferred_element_type=jnp.float32
            )
            if row_max is None:
                total, acc = block_total, term
            else:
                shrink = jnp.exp2(row_max - new_max)
                total = total * shrink + block_total
                acc = acc * shrink + term
            row_max = new_max
    lse = jnp.broadcast_to(jnp.log2(total) + row_max, acc.shape)
    return (acc / total).astype(jnp.bfloat16), lse


def attend_kernel(valid_ref, q_ref, own_ref, other_ref, out_ref, table):
    slots = q_ref.shape[0]

    def note(slot, count):
        is_valid = valid_ref[slot]

        @pl.when(is_valid == 1)
        def _():
            table[count] = slot

        return count + is_valid

    count = lax.fori_loop(0, slots, note, jnp.int32(0))
    for extra in range(GROUP):
        table[count + extra] = table[0]

    kv_refs = (own_ref, other_ref)

    def body(group, carry):
        picks = [table[group * GROUP + i] for i in range(GROUP)]
        full = jnp.concatenate([q_ref[pick, 0:HALF, :] for pick in picks], axis=0)
        out_full, lse_full = attend_rows(full, kv_refs, 0)
        shared = jnp.concatenate([q_ref[pick, HALF:Q_ROWS, :] for pick in picks], axis=0)
        out_shared, lse_shared = attend_rows(shared, kv_refs, 1)
        row_ids = lax.broadcasted_iota(jnp.int32, (16, DEPTH), 0)
        for i, pick in enumerate(picks):
            out_ref[pick, 0:HALF, :] = out_full[i * HALF : (i + 1) * HALF]
            out_ref[pick, HALF:Q_ROWS, :] = out_shared[i * QUART : (i + 1) * QUART]
            lse_one = lse_shared[i * QUART : (i + 1) * QUART]
            pair = (
                jnp.transpose(lse_full[i * HALF : (i + 1) * HALF]),
                jnp.transpose(jnp.concatenate([lse_one, lse_one], axis=0)),
            )
            stats = jnp.zeros((16, DEPTH), jnp.float32)
            for j, lanes in enumerate(pair):
                rest = lanes[0:16]
                for term in range(3):
                    piece = rest.astype(jnp.bfloat16).astype(jnp.float32)
                    rest = rest - piece
                    stats = jnp.where(row_ids == 3 * j + term, piece, stats)
            out_ref[pick, Q_ROWS:SLOT_ROWS, :] = stats.astype(jnp.bfloat16)
        return carry

    lax.fori_loop(0, pl.cdiv(count, GROUP), body, 0)


def attend(valid, queries, own, other):
    slots = queries.shape[0]
    return pl.pallas_call(
        attend_kernel,
        in_specs=[smem(), vmem(), vmem(), vmem()],
        out_specs=vmem(),
        out_shape=jax.ShapeDtypeStruct((slots, SLOT_ROWS, DEPTH), jnp.bfloat16),
        scratch_shapes=[
            pltpu.SMEM((slots + GROUP,), jnp.int32),
        ],
        cost_estimate=cost(20 * 10**9, 8 * MIB),
        compiler_params=pltpu.CompilerParams(vmem_limit_bytes=48 * MIB),
    )(valid, queries, own, other)


def combine_kernel(rows_ref, part_ref, out_ref):
    out_ref[...] = jnp.zeros_like(out_ref)
    band_count = out_ref.shape[0]
    sources = part_ref.shape[0]
    for slot in range(SLOTS):
        row = rows_ref[slot]

        @pl.when(row < band_count)
        def _():
            stats = [
                part_ref[i, slot, Q_ROWS:SLOT_ROWS, :].astype(jnp.float32) for i in range(sources)
            ]
            for j, (first, size) in enumerate(((0, HALF), (HALF, QUART))):
                lses = [s[3 * j : 3 * j + 1] + s[3 * j + 1 : 3 * j + 2] + s[3 * j + 2 : 3 * j + 3] for s in stats]
                top = lses[0]
                for lse in lses[1:]:
                    top = jnp.maximum(top, lse)
                shares = [jnp.exp2(lse - top) for lse in lses]
                whole = shares[0]
                for share in shares[1:]:
                    whole = whole + share
                total = jnp.zeros((size, DEPTH), jnp.float32)
                for i in range(sources):
                    share = jnp.broadcast_to(shares[i] / whole, (DEPTH, DEPTH))
                    total = total + jnp.transpose(share)[0:size] * part_ref[
                        i, slot, first : first + size, :
                    ].astype(jnp.float32)
                out_ref[row, first : first + size, :] = total.astype(jnp.bfloat16)


def combine(listed_rows, partials, band_count):
    return pl.pallas_call(
        combine_kernel,
        in_specs=[smem(), vmem()],
        out_specs=vmem(),
        out_shape=jax.ShapeDtypeStruct((band_count, Q_ROWS, DEPTH), jnp.bfloat16),
        compiler_params=pltpu.CompilerParams(vmem_limit_bytes=24 * MIB),
    )(listed_rows, partials)


def unpack_kernel(in_ref, out_ref):
    for chip in range(in_ref.shape[0]):
        trio, second = chip // 2, chip % 2
        head = 3 * trio + 2 * second
        out_ref[:, head * DEPTH : (head + 1) * DEPTH] = in_ref[chip, 0, 0:HALF, :]
        shared = slice((3 * trio + 1) * DEPTH, (3 * trio + 2) * DEPTH)
        out_ref[second * QUART : (second + 1) * QUART, shared] = in_ref[chip, 0, HALF:Q_ROWS, :]


def unpack(received, features):
    chips = received.shape[0] // 2
    return pl.pallas_call(
        unpack_kernel,
        grid=(2,),
        in_specs=[pl.BlockSpec((chips, 1, Q_ROWS, DEPTH), lambda core: (0, core, 0, 0))],
        out_specs=pl.BlockSpec((HALF, features), lambda core: (core, 0)),
        out_shape=jax.ShapeDtypeStruct((TOKS, features), jnp.bfloat16),
        cost_estimate=cost(0, 2 * 786432),
    )(received.reshape(chips, 2, Q_ROWS, DEPTH))


def per_device(kv_cache, fresh_qkv, edit_list):
    tile_edge, tile_width, _, features = kv_cache.shape
    row_axes = ("chip", "core")
    band_count = lax.axis_size(row_axes)
    col_count = lax.axis_size("col")
    listed_rows = edit_list[:, 0]
    fresh = fresh_qkv.transpose(0, 2, 1, 3)
    message = pack(row_axes, listed_rows, kv_cache, fresh)
    own = lax.all_to_all(message, row_axes, 0, 0, tiled=True)
    other = lax.ppermute(own, "core", [(0, 1), (1, 0)])
    spread = pick(listed_rows, own, col_count)
    queries = lax.all_to_all(spread, "col", 0, 0, tiled=True)
    queries = queries.reshape(col_count * SLOTS, SLOT_ROWS, DEPTH)
    valid = queries[:, Q_ROWS, 0].astype(jnp.int32)

    partials = attend(valid, queries, own, other)
    partials = partials.reshape(col_count, SLOTS, SLOT_ROWS, DEPTH)
    partials = lax.all_to_all(partials, "col", 0, 0, tiled=True)
    finished = combine(listed_rows, partials, band_count)
    finished = lax.all_to_all(finished, row_axes, 0, 0, tiled=True)
    return unpack(finished, features).reshape(tile_edge, tile_width, features)


def solution(mesh):
    rows, cols = mesh.devices.shape
    fine = Mesh(mesh.devices.reshape(rows // 2, 2, cols), ("chip", "core", "col"))
    split = ("chip", "core")
    placed = (P(split, "col", None, None), P(split, "col", None, None), P(None, "col"))
    return jax.shard_map(
        per_device, mesh=fine, in_specs=placed, out_specs=P(split, "col", None), check_vma=False
    )
```

time: 170 us -> 157 us (0.924)
  between operations: 7.4 us -> 0.04 us
  local copies, waits for them, and re-layouts: 8.97 us -> 2.03 us
  Pallas kernels: 29.6 us -> 35.5 us
  other arithmetic: 5.08 us -> 0.66 us
    slice x3 -> x0, local copies, waits for them, and re-layouts: 7.03 us -> none  [the longest x1 4.79 us: per_device(): values = jnp.where(own_edited, fresh_qkv[:, :, 2, :], kv_cache[:, :, 1, :])]
    pallas_call x1, Pallas kernels: 20.8 us -> 27.3 us  [attend(): pl.pallas_call(attend_kernel, in_specs=[smem(), vmem(), vmem(), vmem()],...]
    select_n x1 -> x0, other arithmetic: 3.7 us -> none  [per_device(): values = jnp.where(own_edited, fresh_qkv[:, :, 2, :], kv_cache[:, :, 1, :])]
    pallas_call x2 -> x3, Pallas kernels: 7.48 us -> 7.16 us  [the longest x1 4.46 us: pack(): pl.pallas_call(functools.partial(pack_kernel, row_axes), grid=(4,), in_sp...]
  transfers between devices with their start and end apart: 1 -> 1, of which waited for: 0 -> 0; matrix products, arithmetic and copies ran while one was open for 2% -> 0% of each run, Pallas kernels for 0% -> 0%
where the time goes in v2:
time: 157 us
  blocking collectives  118 us (75%)
  Pallas kernels  35.5 us (23%)
  local copies, waits for them, and re-layouts  2.03 us (1%)
    all_to_all x1, blocking collectives, per_device(): own = lax.all_to_all(message, row_axes, 0, 0, tiled=True)  43.4 us
    all_to_all x1, blocking collectives, per_device(): queries = lax.all_to_all(spread, 'col', 0, 0, tiled=True)  30.8 us
    pallas_call x1, Pallas kernels, attend(): pl.pallas_call(attend_kernel, in_specs=[smem(), vmem(), vmem(), vmem()],...  27.3 us
    all_to_all x1, blocking collectives, per_device(): partials = lax.all_to_all(partials, 'col', 0, 0, tiled=True)  25.1 us
    all_to_all x1, blocking collectives, per_device(): finished = lax.all_to_all(finished, row_axes, 0, 0, tiled=True)  18.7 us
    pallas_call x1, Pallas kernels, pack(): pl.pallas_call(functools.partial(pack_kernel, row_axes), grid=(4,), in_sp...  4.46 us
  transfers between devices with their start and end apart: 1, of which 0 were waited for; matrix products, arithmetic and copies ran while one was open for 0% of the time, Pallas kernels for 0%

profile of v2, /device:TPU:1, one launch (start us, length us, event | category | flops | bytes accessed | tf_op | source)
XLA Modules:
  0.0 156.6 jit_solution(11405196614103505169)
XLA Ops:
  0.0 4.5 %shard_map.37 = bf16[16,704,128]{2,1,0:T(8,128)(2,1)} custom-call(s32[4]{0:T(128)} %bitcast.9, bf16[16,16,2,1536]{3,2,1,0:T(2,128)(2,1)} %cache_ref.1, bf16[16,3,16,1536]{3,2,1,0:T(8,128)(2,1)} %bitcast.12, bf16[16,3,16,1536]{3,2,1,0:T(8,128)(2,1)} %bitcast.13, bf16[16,3,16,1536]{3,2,1,0:T(8,128)(2,1)} %bitcast.14), custom_call_target="tpu_custom_call" | custom-call | bytes 7077888 | tf_op jit(solution)/shard_map/pallas_call | solution.py:95
  4.5 0.0 copy-start.1
  4.5 43.4 %all_to_all.20.got_ref.own_ref = bf16[16,704,128]{2,1,0:T(8,128)(2,1)S(1)} all-to-all(bf16[16,704,128]{2,1,0:T(8,128)(2,1)} %shard_map.37), channel_id=1, replica_groups=mesh['chip'=8,'core'=2,'col'=8] {'chip','core'}, dimensions={0} | all-to-all | bytes 5767168 | tf_op jit(solution)/shard_map/all_to_all | solution.py:297
  47.9 0.0 copy-start
  47.9 0.4 collective-permute-start
  48.3 0.0 copy-done.1
  48.3 0.8 shard_map.38
  49.1 0.4 copy-done
  49.5 30.8 %all_to_all.21 = bf16[8,4,208,128]{3,2,1,0:T(8,128)(2,1)S(1)} all-to-all(bf16[8,4,208,128]{3,2,1,0:T(8,128)(2,1)S(1)} %shard_map.38), channel_id=1, replica_groups=mesh['chip'=8,'core'=2,'col'=8] {'col'}, dimensions={0} | all-to-all | bytes 3407872 | tf_op jit(solution)/shard_map/all_to_all | solution.py:300
  80.3 0.7 fusion.valid_ref
  81.0 0.0 collective-permute-done.other_ref
  81.0 0.0 copy-start.2
  81.0 1.6 %copy-done.2 = bf16[16,704,128]{2,1,0:T(8,128)(2,1)} copy-done((bf16[16,704,128]{2,1,0:T(8,128)(2,1)}, bf16[16,704,128]{2,1,0:T(8,128)(2,1)S(1)}, u32[]{:S(2)}) %copy-start.2) | copy-done | bytes 2883608
  82.6 27.3 %shard_map.39 = bf16[32,208,128]{2,1,0:T(8,128)(2,1)S(1)} custom-call(s32[32]{0:T(128)S(1)} %fusion.valid_ref, bf16[32,208,128]{2,1,0:T(8,128)(2,1)S(1)} %bitcast.7, bf16[16,704,128]{2,1,0:T(8,128)(2,1)} %copy-done, bf16[16,704,128]{2,1,0:T(8,128)(2,1)} %copy-done.2), custom_call_target="tpu_custom_call" | custom-call | flops 20000000000 | bytes 8388608 | tf_op jit(solution)/shard_map/pallas_call | solution.py:215
  109.9 25.1 %all_to_all.22.part_ref = bf16[8,4,208,128]{3,2,1,0:T(8,128)(2,1)S(1)} all-to-all(bf16[8,4,208,128]{3,2,1,0:T(8,128)(2,1)S(1)} %bitcast.8), channel_id=1, replica_groups=mesh['chip'=8,'core'=2,'col'=8] {'col'}, dimensions={0} | all-to-all | bytes 3407872 | tf_op jit(solution)/shard_map/all_to_all | solution.py:306
  135.0 1.0 shard_map.40
  136.0 18.7 %all_to_all.23 = bf16[16,192,128]{2,1,0:T(8,128)(2,1)} all-to-all(bf16[16,192,128]{2,1,0:T(8,128)(2,1)S(1)} %shard_map.40), channel_id=1, replica_groups=mesh['chip'=8,'core'=2,'col'=8] {'chip','core'}, dimensions={0} | all-to-all | bytes 1572864 | tf_op jit(solution)/shard_map/all_to_all | solution.py:308
  154.7 1.9 %shard_map.41 = bf16[256,1536]{1,0:T(8,128)(2,1)} custom-call(bf16[8,2,192,128]{3,2,1,0:T(8,128)(2,1)} %bitcast.15), custom_call_target="tpu_custom_call" | custom-call | bytes 1572864 | tf_op jit(solution)/shard_map/pallas_call | solution.py:279
Async XLA Ops:
  4.5 43.9 %copy-start.1 = (s32[4,1]{0,1:T(1,128)S(1)}, s32[4,1]{0,1:T(1,128)}, u32[]{:S(2)}) copy-start(s32[4,1]{0,1:T(1,128)} %param.5) | copy-start | bytes 52
  47.9 1.6 %copy-start = (bf16[16,704,128]{2,1,0:T(8,128)(2,1)}, bf16[16,704,128]{2,1,0:T(8,128)(2,1)S(1)}, u32[]{:S(2)}) copy-start(bf16[16,704,128]{2,1,0:T(8,128)(2,1)S(1)} %all_to_all.20.got_ref.own_ref) | copy-start | bytes 8650756
  47.9 33.0 %collective-permute-start = (bf16[16,704,128]{2,1,0:T(8,128)(2,1)S(1)}, bf16[16,704,128]{2,1,0:T(8,128)(2,1)S(1)}, u32[]{:S(2)}, u32[]{:S(2)}) collective-permute-start(bf16[16,704,128]{2,1,0:T(8,128)(2,1)S(1)} %all_to_all.20.got_ref.own_ref), channel_id=1, source_target_pairs={{0,8},{8,0},{1,9},{9,1},{2,10},{10,2},{3,11},{11,3},{4,12},{12,4},... | collective-permute-start | bytes 8650760 | tf_op jit(solution)/shard_map/ppermute | solution.py:298
  81.0 1.6 %copy-start.2 = (bf16[16,704,128]{2,1,0:T(8,128)(2,1)}, bf16[16,704,128]{2,1,0:T(8,128)(2,1)S(1)}, u32[]{:S(2)}) copy-start(bf16[16,704,128]{2,1,0:T(8,128)(2,1)S(1)} %collective-permute-done.other_ref) | copy-start | bytes 8650756

commit v3 on v2

--- a/solution.py
+++ b/solution.py
@@ -132,39 +132,58 @@
     )(listed_rows, received)
 
 
-def attend_rows(queries, kv_refs, head):
+def widen_kernel(own_ref, other_ref, out_ref):
+    for head in range(2):
+        first = 2 * HALF * head + HALF
+        for part, kv_ref in enumerate((own_ref, other_ref)):
+            rows = slice(part * 2048, (part + 1) * 2048)
+            out_ref[head, rows, 0:DEPTH] = kv_ref[:, first : first + HALF, :].reshape(2048, DEPTH)
+        out_ref[head, :, DEPTH:] = jnp.ones((4096, DEPTH), jnp.bfloat16)
+
+
+def widen(own, other):
+    return pl.pallas_call(
+        widen_kernel,
+        in_specs=[vmem(), vmem()],
+        out_specs=vmem(),
+        out_shape=jax.ShapeDtypeStruct((2, 4096, 2 * DEPTH), jnp.bfloat16),
+        cost_estimate=cost(0, 8 * MIB),
+        compiler_params=pltpu.CompilerParams(vmem_limit_bytes=16 * MIB),
+    )(own, other)
+
+
+def attend_rows(queries, kv_refs, values_ref, head):
     fold = math.log2(math.e) / math.sqrt(DEPTH)
-    row_max = total = acc = None
+    row_max = acc = None
     tiles = KEY_BLOCK // HALF
     first = 2 * HALF * head
-    for kv_ref in kv_refs:
+    for part, kv_ref in enumerate(kv_refs):
         for block in range(kv_ref.shape[0] // tiles):
             rows = slice(block * tiles, (block + 1) * tiles)
             keys = kv_ref[rows, first : first + HALF, :].reshape(KEY_BLOCK, DEPTH)
-            values = kv_ref[rows, first + HALF : first + 2 * HALF, :].reshape(KEY_BLOCK, DEPTH)
             scores = lax.dot_general(
                 queries, keys, (((1,), (1,)), ((), ())), preferred_element_type=jnp.float32
             )
             scores = scores * fold
             block_max = jnp.max(scores, axis=1, keepdims=True)
             new_max = block_max if row_max is None else jnp.maximum(row_max, block_max)
-            weights = jnp.exp2(scores - new_max)
-            block_total = jnp.sum(weights, axis=1, keepdims=True)
+            weights = jnp.exp2(scores - new_max).astype(jnp.bfloat16)
+            start = part * 2048 + block * KEY_BLOCK
             term = jnp.dot(
-                weights.astype(jnp.bfloat16), values, preferred_element_type=jnp.float32
+                weights,
+                values_ref[head, start : start + KEY_BLOCK, :],
+                preferred_element_type=jnp.float32,
             )
             if row_max is None:
-                total, acc = block_total, term
+                acc = term
             else:
-                shrink = jnp.exp2(row_max - new_max)
-                total = total * shrink + block_total
-                acc = acc * shrink + term
+                acc = acc * jnp.exp2(row_max - new_max) + term
             row_max = new_max
-    lse = jnp.broadcast_to(jnp.log2(total) + row_max, acc.shape)
-    return (acc / total).astype(jnp.bfloat16), lse
-
-
-def attend_kernel(valid_ref, q_ref, own_ref, other_ref, out_ref, table):
+    total = acc[:, DEPTH:]
+    return (acc[:, :DEPTH] / total).astype(jnp.bfloat16), jnp.log2(total) + row_max
+
+
+def attend_kernel(valid_ref, q_ref, own_ref, other_ref, values_ref, out_ref, table):
     slots = q_ref.shape[0]
 
     def note(slot, count):
@@ -182,12 +201,12 @@
 
     kv_refs = (own_ref, other_ref)
 
-    def body(group, carry):
-        picks = [table[group * GROUP + i] for i in range(GROUP)]
+    def attend_tiles(start, size):
+        picks = [table[start + i] for i in range(size)]
         full = jnp.concatenate([q_ref[pick, 0:HALF, :] for pick in picks], axis=0)
-        out_full, lse_full = attend_rows(full, kv_refs, 0)
+        out_full, lse_full = attend_rows(full, kv_refs, values_ref, 0)
         shared = jnp.concatenate([q_ref[pick, HALF:Q_ROWS, :] for pick in picks], axis=0)
-        out_shared, lse_shared = attend_rows(shared, kv_refs, 1)
+        out_shared, lse_shared = attend_rows(shared, kv_refs, values_ref, 1)
         row_ids = lax.broadcasted_iota(jnp.int32, (16, DEPTH), 0)
         for i, pick in enumerate(picks):
             out_ref[pick, 0:HALF, :] = out_full[i * HALF : (i + 1) * HALF]
@@ -205,24 +224,31 @@
                     rest = rest - piece
                     stats = jnp.where(row_ids == 3 * j + term, piece, stats)
             out_ref[pick, Q_ROWS:SLOT_ROWS, :] = stats.astype(jnp.bfloat16)
+
+    groups = (count + 1) // GROUP
+
+    def body(group, carry):
+        attend_tiles(group * GROUP, GROUP)
         return carry
 
-    lax.fori_loop(0, pl.cdiv(count, GROUP), body, 0)
-
-
-def attend(valid, queries, own, other):
+    lax.fori_loop(0, groups, body, 0)
+
+    @pl.when(groups * GROUP < count)
+    def _():
+        attend_tiles(groups * GROUP, 2)
+
+
+def attend(valid, queries, own, other, values):
     slots = queries.shape[0]
     return pl.pallas_call(
         attend_kernel,
-        in_specs=[smem(), vmem(), vmem(), vmem()],
+        in_specs=[smem(), vmem(), vmem(), vmem(), vmem()],
         out_specs=vmem(),
         out_shape=jax.ShapeDtypeStruct((slots, SLOT_ROWS, DEPTH), jnp.bfloat16),
-        scratch_shapes=[
-            pltpu.SMEM((slots + GROUP,), jnp.int32),
-        ],
+        scratch_shapes=[pltpu.SMEM((slots + GROUP,), jnp.int32)],
         cost_estimate=cost(20 * 10**9, 8 * MIB),
-        compiler_params=pltpu.CompilerParams(vmem_limit_bytes=48 * MIB),
-    )(valid, queries, own, other)
+        compiler_params=pltpu.CompilerParams(vmem_limit_bytes=40 * MIB),
+    )(valid, queries, own, other, values)
 
 
 def combine_kernel(rows_ref, part_ref, out_ref):
@@ -301,7 +327,7 @@
     queries = queries.reshape(col_count * SLOTS, SLOT_ROWS, DEPTH)
     valid = queries[:, Q_ROWS, 0].astype(jnp.int32)
 
-    partials = attend(valid, queries, own, other)
+    partials = attend(valid, queries, own, other, widen(own, other))
     partials = partials.reshape(col_count, SLOTS, SLOT_ROWS, DEPTH)
     partials = lax.all_to_all(partials, "col", 0, 0, tiled=True)
     finished = combine(listed_rows, partials, band_count)

time: 157 us -> 147 us (0.936)
  Pallas kernels: 35.5 us -> 28 us
  local copies, waits for them, and re-layouts: 2.03 us -> 0.01 us
    pallas_call x1 -> x2, Pallas kernels: 27.3 us -> 18.3 us  [the longest x1 17.7 us: attend(): pl.pallas_call(attend_kernel, in_specs=[smem(), vmem(), vmem(), vmem(), v...]
    unnamed x6 -> x2, local copies, waits for them, and re-layouts: 2.03 us -> 0.01 us
  transfers between devices with their start and end apart: 1 -> 1, of which waited for: 0 -> 0; matrix products, arithmetic and copies ran while one was open for 0% -> 0% of each run, Pallas kernels for 0% -> 1%
where the time goes in v3:
time: 147 us
  blocking collectives  118 us (80%)
  Pallas kernels  28 us (19%)
    all_to_all x1, blocking collectives, per_device(): own = lax.all_to_all(message, row_axes, 0, 0, tiled=True)  42.8 us
    all_to_all x1, blocking collectives, per_device(): queries = lax.all_to_all(spread, 'col', 0, 0, tiled=True)  31.1 us
    all_to_all x1, blocking collectives, per_device(): partials = lax.all_to_all(partials, 'col', 0, 0, tiled=True)  25.1 us
    all_to_all x1, blocking collectives, per_device(): finished = lax.all_to_all(finished, row_axes, 0, 0, tiled=True)  18.6 us
    pallas_call x1, Pallas kernels, attend(): pl.pallas_call(attend_kernel, in_specs=[smem(), vmem(), vmem(), vmem(), v...  17.7 us
    pallas_call x1, Pallas kernels, pack(): pl.pallas_call(functools.partial(pack_kernel, row_axes), grid=(4,), in_sp...  4.94 us
  transfers between devices with their start and end apart: 1, of which 0 were waited for; matrix products, arithmetic and copies ran while one was open for 0% of the time, Pallas kernels for 1%

profile of v3, /device:TPU:1, one launch (start us, length us, event | category | flops | bytes accessed | tf_op | source)
XLA Modules:
  0.0 146.8 jit_solution(10843418016770801212)
XLA Ops:
  0.0 4.9 %shard_map.37 = bf16[16,704,128]{2,1,0:T(8,128)(2,1)} custom-call(s32[4]{0:T(128)} %bitcast.9, bf16[16,16,2,1536]{3,2,1,0:T(2,128)(2,1)} %cache_ref.1, bf16[16,3,16,1536]{3,2,1,0:T(8,128)(2,1)} %bitcast.12, bf16[16,3,16,1536]{3,2,1,0:T(8,128)(2,1)} %bitcast.13, bf16[16,3,16,1536]{3,2,1,0:T(8,128)(2,1)} %bitcast.14), custom_call_target="tpu_custom_call" | custom-call | bytes 7077888 | tf_op jit(solution)/shard_map/pallas_call | solution.py:95
  4.9 0.0 copy-start
  4.9 42.8 %all_to_all.20.got_ref.own_ref = bf16[16,704,128]{2,1,0:T(8,128)(2,1)S(1)} all-to-all(bf16[16,704,128]{2,1,0:T(8,128)(2,1)} %shard_map.37), channel_id=1, replica_groups=mesh['chip'=8,'core'=2,'col'=8] {'chip','core'}, dimensions={0} | all-to-all | bytes 5767168 | tf_op jit(solution)/shard_map/all_to_all | solution.py:323
  47.7 0.4 collective-permute-start
  48.1 0.0 copy-done
  48.1 0.8 shard_map.38
  48.9 31.1 %all_to_all.21 = bf16[8,4,208,128]{3,2,1,0:T(8,128)(2,1)S(1)} all-to-all(bf16[8,4,208,128]{3,2,1,0:T(8,128)(2,1)S(1)} %shard_map.38), channel_id=1, replica_groups=mesh['chip'=8,'core'=2,'col'=8] {'col'}, dimensions={0} | all-to-all | bytes 3407872 | tf_op jit(solution)/shard_map/all_to_all | solution.py:326
  80.0 0.7 fusion.valid_ref
  80.7 0.0 collective-permute-done.other_ref
  80.7 0.6 shard_map.39.values_ref
  81.3 17.7 %shard_map.40 = bf16[32,208,128]{2,1,0:T(8,128)(2,1)S(1)} custom-call(s32[32]{0:T(128)S(1)} %fusion.valid_ref, bf16[32,208,128]{2,1,0:T(8,128)(2,1)S(1)} %bitcast.7, bf16[16,704,128]{2,1,0:T(8,128)(2,1)S(1)} %all_to_all.20.got_ref.own_ref, bf16[16,704,128]{2,1,0:T(8,128)(2,1)S(1)} %collective-permute-done.other_ref, ...), custom_call_target="tpu_custom_call" | custom-call | flops 20000000000 | bytes 8388608 | tf_op jit(solution)/shard_map/pallas_call | solution.py:243
  99.0 25.1 %all_to_all.22.part_ref = bf16[8,4,208,128]{3,2,1,0:T(8,128)(2,1)S(1)} all-to-all(bf16[8,4,208,128]{3,2,1,0:T(8,128)(2,1)S(1)} %bitcast.8), channel_id=1, replica_groups=mesh['chip'=8,'core'=2,'col'=8] {'col'}, dimensions={0} | all-to-all | bytes 3407872 | tf_op jit(solution)/shard_map/all_to_all | solution.py:332
  124.1 2.1 %shard_map.41 = bf16[16,192,128]{2,1,0:T(8,128)(2,1)S(1)} custom-call(s32[4]{0:T(128)S(1)} %bitcast.11, bf16[8,4,208,128]{3,2,1,0:T(8,128)(2,1)S(1)} %all_to_all.22.part_ref), custom_call_target="tpu_custom_call" | custom-call | tf_op jit(solution)/shard_map/pallas_call | solution.py:285
  126.2 18.6 %all_to_all.23 = bf16[16,192,128]{2,1,0:T(8,128)(2,1)} all-to-all(bf16[16,192,128]{2,1,0:T(8,128)(2,1)S(1)} %shard_map.41), channel_id=1, replica_groups=mesh['chip'=8,'core'=2,'col'=8] {'chip','core'}, dimensions={0} | all-to-all | bytes 1572864 | tf_op jit(solution)/shard_map/all_to_all | solution.py:334
  144.9 1.9 %shard_map.42 = bf16[256,1536]{1,0:T(8,128)(2,1)} custom-call(bf16[8,2,192,128]{3,2,1,0:T(8,128)(2,1)} %bitcast.15), custom_call_target="tpu_custom_call" | custom-call | bytes 1572864 | tf_op jit(solution)/shard_map/pallas_call | solution.py:305
Async XLA Ops:
  4.9 43.2 %copy-start = (s32[4,1]{0,1:T(1,128)S(1)}, s32[4,1]{0,1:T(1,128)}, u32[]{:S(2)}) copy-start(s32[4,1]{0,1:T(1,128)} %param.5) | copy-start | bytes 52
  47.7 33.0 %collective-permute-start = (bf16[16,704,128]{2,1,0:T(8,128)(2,1)S(1)}, bf16[16,704,128]{2,1,0:T(8,128)(2,1)S(1)}, u32[]{:S(2)}, u32[]{:S(2)}) collective-permute-start(bf16[16,704,128]{2,1,0:T(8,128)(2,1)S(1)} %all_to_all.20.got_ref.own_ref), channel_id=1, source_target_pairs={{0,8},{8,0},{1,9},{9,1},{2,10},{10,2},{3,11},{11,3},{4,12},{12,4},... | collective-permute-start | bytes 8650760 | tf_op jit(solution)/shard_map/ppermute | solution.py:324

commit v4 on v3

--- a/solution.py
+++ b/solution.py
@@ -1,4 +1,3 @@
-import functools
 import math
 
 import jax
@@ -13,9 +12,8 @@
 TOKS = 256
 HALF = 128
 QUART = 64
-KV_ROWS = 4 * HALF
+KV_ROWS = 4 * TOKS
 Q_ROWS = HALF + QUART
-MSG_ROWS = KV_ROWS + Q_ROWS
 SLOT_ROWS = Q_ROWS + 16
 GROUP = 4
 KEY_BLOCK = 512
@@ -30,51 +28,71 @@
     return pl.BlockSpec(memory_space=pltpu.SMEM)
 
 
+CHIP = ("y", "z_lo")
+ROW = CHIP + ("core",)
+
+
+STEPS = (5, 4, 7, 2, 3, 6, 1)
+
+
+def flip():
+    return lax.axis_index("col") // (lax.axis_size("col") // 2)
+
+
+def across(x):
+    cols = lax.axis_size("col")
+    near, far = list(range(cols // 2)), list(range(cols // 2, cols))
+    groups = [near + [cols + i for i in far], [cols + i for i in near] + far]
+    return lax.all_to_all(x, ("z_lo", "col"), 0, 0, axis_index_groups=groups, tiled=True)
+
+
 def cost(flops, moved):
     return pl.CostEstimate(flops=flops, bytes_accessed=moved, transcendentals=0)
 
 
+def pack_query_kernel(in_ref, out_ref):
+    for chip in range(out_ref.shape[0]):
+        trio, second = chip // 2, chip % 2
+        head = 3 * trio + 2 * second
+        dest = jnp.bitwise_xor(chip, flip())
+        out_ref[dest, 0, 0:HALF, :] = in_ref[:, 0, :, head * DEPTH : (head + 1) * DEPTH].reshape(
+            HALF, DEPTH
+        )
+        shared = slice((3 * trio + 1) * DEPTH, (3 * trio + 2) * DEPTH)
+        rows = slice(second * 4, second * 4 + 4)
+        out_ref[dest, 0, HALF:Q_ROWS, :] = in_ref[rows, 0, :, shared].reshape(QUART, DEPTH)
+
+
+def pack_query(fresh, chips):
+    features = fresh.shape[3]
+    out = pl.pallas_call(
+        pack_query_kernel,
+        grid=(2,),
+        in_specs=[pl.BlockSpec((8, 1, 16, features), lambda core: (core, 0, 0, 0))],
+        out_specs=pl.BlockSpec((chips, 1, Q_ROWS, DEPTH), lambda core: (0, core, 0, 0)),
+        out_shape=jax.ShapeDtypeStruct((chips, 2, Q_ROWS, DEPTH), jnp.bfloat16),
+        cost_estimate=cost(0, 2 * 786432),
+    )(fresh)
+    return out.reshape(2 * chips, Q_ROWS, DEPTH)
+
+
 def fresh_spec(part):
     return pl.BlockSpec((16, 1, 16, 3 * DEPTH), lambda p: (0, part, 0, p))
 
 
-def pack_kernel(row_axes, rows_ref, cache_ref, query_ref, keys_ref, values_ref, out_ref):
-    my_row = lax.axis_index(row_axes)
+def pack_kernel(rows_ref, cache_ref, keys_ref, values_ref, *refs):
+    out_refs, sorted_ref = refs[:-1], refs[-1]
+    my_chip = lax.axis_index(CHIP)
+    my_row = 2 * my_chip + lax.axis_index("core")
+    my_chip = jnp.bitwise_xor(my_chip, flip())
     edited = rows_ref[0] == my_row
     for slot in range(1, SLOTS):
         edited = jnp.logical_or(edited, rows_ref[slot] == my_row)
 
-    def place(core, head, keys, values):
-        for chip in ((0,), (0, 1), (1,))[head]:
-            first = 2 * HALF if head == 1 else 0
-            out_ref[chip * 2 + core, first : first + HALF, :] = keys
-            out_ref[chip * 2 + core, first + HALF : first + 2 * HALF, :] = values
-
-    for chip in range(2):
-        full = slice(0, DEPTH) if chip == 0 else slice(2 * DEPTH, 3 * DEPTH)
-        for core in range(2):
-            dest = chip * 2 + core
-            rows = slice(core * 8, core * 8 + 8)
-            quart = slice(core * 8 + chip * 4, core * 8 + chip * 4 + 4)
-            out_ref[dest, KV_ROWS : KV_ROWS + HALF, :] = query_ref[rows, 0, :, full].reshape(
-                HALF, DEPTH
-            )
-            out_ref[dest, KV_ROWS + HALF : MSG_ROWS, :] = query_ref[
-                quart, 0, :, DEPTH : 2 * DEPTH
-            ].reshape(QUART, DEPTH)
-
     @pl.when(edited)
     def _():
-        for core in range(2):
-            rows = slice(core * 8, core * 8 + 8)
-            for head in range(3):
-                cols = slice(head * DEPTH, (head + 1) * DEPTH)
-                place(
-                    core,
-                    head,
-                    keys_ref[rows, 0, :, cols].reshape(HALF, DEPTH),
-                    values_ref[rows, 0, :, cols].reshape(HALF, DEPTH),
-                )
+        for part, ref in enumerate((keys_ref, values_ref)):
+            sorted_ref[part] = ref[...].reshape(TOKS, 3 * DEPTH)
 
     @pl.when(jnp.logical_not(edited))
     def _():
@@ -82,38 +100,79 @@
         source_id = lax.broadcasted_iota(jnp.int32, (TOKS, TOKS), 1)
         wanted = jnp.where(place_id < HALF, 2 * place_id, 2 * place_id - (TOKS - 1))
         sorter = (source_id == wanted).astype(jnp.float32).astype(jnp.bfloat16)
-        for core in range(2):
-            pairs = cache_ref[core * 8 : core * 8 + 8].reshape(TOKS, 3 * DEPTH)
+        for half in range(2):
+            pairs = cache_ref[half * 8 : half * 8 + 8].reshape(TOKS, 3 * DEPTH)
             apart = jnp.dot(sorter, pairs, preferred_element_type=jnp.float32)
             apart = apart.astype(jnp.bfloat16)
-            for head in range(3):
-                cols = slice(head * DEPTH, (head + 1) * DEPTH)
-                place(core, head, apart[0:HALF, cols], apart[HALF:TOKS, cols])
-
-
-def pack(row_axes, listed_rows, cache, fresh):
-    return pl.pallas_call(
-        functools.partial(pack_kernel, row_axes),
-        grid=(4,),
+            for part in range(2):
+                sorted_ref[part, half * HALF : (half + 1) * HALF, :] = apart[
+                    part * HALF : (part + 1) * HALF
+                ]
+
+    pair = jnp.bitwise_xor(pl.program_id(0), my_chip // 2)
+    swapped = jnp.bitwise_and(my_chip, 1)
+    for j in range(len(out_refs) // 2):
+        for i in range(2):
+            second = jnp.bitwise_xor(swapped, i)
+
+            for which in range(2):
+
+                @pl.when(jnp.logical_and(pair == j, second == which))
+                def _():
+                    full = slice(2 * which * DEPTH, (2 * which + 1) * DEPTH)
+                    out_ref = out_refs[((0,) + STEPS).index(2 * j + i)]
+                    for part in range(2):
+                        out_ref[part * TOKS : (part + 1) * TOKS, :] = sorted_ref[part, :, full]
+                        out_ref[(2 + part) * TOKS : (3 + part) * TOKS, :] = sorted_ref[
+                            part, :, DEPTH : 2 * DEPTH
+                        ]
+
+
+def pack(listed_rows, cache, fresh, chips):
+    return pl.pallas_call(
+        pack_kernel,
+        grid=(chips // 2,),
         in_specs=[
             smem(),
             pl.BlockSpec((16, 16, 2, 3 * DEPTH), lambda p: (0, 0, 0, p)),
-            fresh_spec(0),
             fresh_spec(1),
             fresh_spec(2),
         ],
-        out_specs=pl.BlockSpec((4, MSG_ROWS, DEPTH), lambda p: (p, 0, 0)),
-        out_shape=jax.ShapeDtypeStruct((16, MSG_ROWS, DEPTH), jnp.bfloat16),
-        cost_estimate=cost(0, 9 * 786432),
-        compiler_params=pltpu.CompilerParams(vmem_limit_bytes=56 * MIB),
-    )(listed_rows, cache, fresh, fresh, fresh)
+        out_specs=[vmem()] * chips,
+        out_shape=[jax.ShapeDtypeStruct((KV_ROWS, DEPTH), jnp.bfloat16)] * chips,
+        scratch_shapes=[pltpu.VMEM((2, TOKS, 3 * DEPTH), jnp.bfloat16)],
+        cost_estimate=cost(0, 7 * 786432),
+        compiler_params=pltpu.CompilerParams(vmem_limit_bytes=20 * MIB),
+    )(listed_rows, cache, fresh, fresh)
+
+
+def join_kernel(*refs):
+    count = len(refs) - 2
+    out_ref, arrived = refs[count], refs[count + 1]
+    copies = [pltpu.make_async_copy(refs[i], out_ref.at[i], arrived.at[i]) for i in range(count)]
+    for copy in copies:
+        copy.start()
+    for copy in copies:
+        copy.wait()
+
+
+def join(pieces):
+    return pl.pallas_call(
+        join_kernel,
+        in_specs=[pl.BlockSpec(memory_space=pl.ANY)] * len(pieces),
+        out_specs=vmem(),
+        out_shape=jax.ShapeDtypeStruct((len(pieces), KV_ROWS, DEPTH), jnp.bfloat16),
+        scratch_shapes=[pltpu.SemaphoreType.DMA((len(pieces),))],
+        cost_estimate=cost(0, 4 * MIB),
+        compiler_params=pltpu.CompilerParams(vmem_limit_bytes=16 * MIB),
+    )(*pieces)
 
 
 def pick_kernel(rows_ref, got_ref, out_ref):
     bands = got_ref.shape[0]
     for slot in range(SLOTS):
         row = rows_ref[slot]
-        rows = got_ref[jnp.minimum(row, bands - 1), KV_ROWS:MSG_ROWS, :]
+        rows = got_ref[jnp.minimum(row, bands - 1)]
         flag = jnp.where(row < bands, 1.0, 0.0)
         flags = jnp.full((SLOT_ROWS - Q_ROWS, DEPTH), flag, jnp.float32).astype(jnp.bfloat16)
         for dest in range(out_ref.shape[0]):
@@ -134,10 +193,10 @@
 
 def widen_kernel(own_ref, other_ref, out_ref):
     for head in range(2):
-        first = 2 * HALF * head + HALF
+        first = 2 * TOKS * head + TOKS
         for part, kv_ref in enumerate((own_ref, other_ref)):
             rows = slice(part * 2048, (part + 1) * 2048)
-            out_ref[head, rows, 0:DEPTH] = kv_ref[:, first : first + HALF, :].reshape(2048, DEPTH)
+            out_ref[head, rows, 0:DEPTH] = kv_ref[:, first : first + TOKS, :].reshape(2048, DEPTH)
         out_ref[head, :, DEPTH:] = jnp.ones((4096, DEPTH), jnp.bfloat16)
 
 
@@ -155,12 +214,12 @@
 def attend_rows(queries, kv_refs, values_ref, head):
     fold = math.log2(math.e) / math.sqrt(DEPTH)
     row_max = acc = None
-    tiles = KEY_BLOCK // HALF
-    first = 2 * HALF * head
+    tiles = KEY_BLOCK // TOKS
+    first = 2 * TOKS * head
     for part, kv_ref in enumerate(kv_refs):
         for block in range(kv_ref.shape[0] // tiles):
             rows = slice(block * tiles, (block + 1) * tiles)
-            keys = kv_ref[rows, first : first + HALF, :].reshape(KEY_BLOCK, DEPTH)
+            keys = kv_ref[rows, first : first + TOKS, :].reshape(KEY_BLOCK, DEPTH)
             scores = lax.dot_general(
                 queries, keys, (((1,), (1,)), ((), ())), preferred_element_type=jnp.float32
             )
@@ -247,7 +306,7 @@
         out_shape=jax.ShapeDtypeStruct((slots, SLOT_ROWS, DEPTH), jnp.bfloat16),
         scratch_shapes=[pltpu.SMEM((slots + GROUP,), jnp.int32)],
         cost_estimate=cost(20 * 10**9, 8 * MIB),
-        compiler_params=pltpu.CompilerParams(vmem_limit_bytes=40 * MIB),
+        compiler_params=pltpu.CompilerParams(vmem_limit_bytes=30 * MIB),
     )(valid, queries, own, other, values)
 
 
@@ -295,9 +354,10 @@
     for chip in range(in_ref.shape[0]):
         trio, second = chip // 2, chip % 2
         head = 3 * trio + 2 * second
-        out_ref[:, head * DEPTH : (head + 1) * DEPTH] = in_ref[chip, 0, 0:HALF, :]
+        source = jnp.bitwise_xor(chip, flip())
+        out_ref[:, head * DEPTH : (head + 1) * DEPTH] = in_ref[source, 0, 0:HALF, :]
         shared = slice((3 * trio + 1) * DEPTH, (3 * trio + 2) * DEPTH)
-        out_ref[second * QUART : (second + 1) * QUART, shared] = in_ref[chip, 0, HALF:Q_ROWS, :]
+        out_ref[second * QUART : (second + 1) * QUART, shared] = in_ref[source, 0, HALF:Q_ROWS, :]
 
 
 def unpack(received, features):
@@ -314,32 +374,40 @@
 
 def per_device(kv_cache, fresh_qkv, edit_list):
     tile_edge, tile_width, _, features = kv_cache.shape
-    row_axes = ("chip", "core")
-    band_count = lax.axis_size(row_axes)
+    band_count = lax.axis_size(ROW)
     col_count = lax.axis_size("col")
     listed_rows = edit_list[:, 0]
     fresh = fresh_qkv.transpose(0, 2, 1, 3)
-    message = pack(row_axes, listed_rows, kv_cache, fresh)
-    own = lax.all_to_all(message, row_axes, 0, 0, tiled=True)
+    chips = lax.axis_size(CHIP)
+    query_message = pack_query(fresh, chips)
+    got_query = lax.all_to_all(query_message, ROW, 0, 0, tiled=True)
+    fresh, query_message = lax.optimization_barrier((fresh, query_message))
+    messages = pack(listed_rows, kv_cache, fresh, chips)
+    spread = pick(listed_rows, got_query, col_count)
+    messages, spread = lax.optimization_barrier((messages, spread))
+    pieces = [messages[0]]
+    for step, message in zip(STEPS, messages[1:]):
+        pairs = [(i, i ^ step) for i in range(chips)]
+        pieces.append(lax.ppermute(message, CHIP, pairs))
+    queries = across(spread)
+    pieces, queries = lax.optimization_barrier((pieces, queries))
+    own = join(pieces)
     other = lax.ppermute(own, "core", [(0, 1), (1, 0)])
-    spread = pick(listed_rows, own, col_count)
-    queries = lax.all_to_all(spread, "col", 0, 0, tiled=True)
     queries = queries.reshape(col_count * SLOTS, SLOT_ROWS, DEPTH)
     valid = queries[:, Q_ROWS, 0].astype(jnp.int32)
 
     partials = attend(valid, queries, own, other, widen(own, other))
     partials = partials.reshape(col_count, SLOTS, SLOT_ROWS, DEPTH)
-    partials = lax.all_to_all(partials, "col", 0, 0, tiled=True)
+    partials = across(partials)
     finished = combine(listed_rows, partials, band_count)
-    finished = lax.all_to_all(finished, row_axes, 0, 0, tiled=True)
+    finished = lax.all_to_all(finished, ROW, 0, 0, tiled=True)
     return unpack(finished, features).reshape(tile_edge, tile_width, features)
 
 
 def solution(mesh):
     rows, cols = mesh.devices.shape
-    fine = Mesh(mesh.devices.reshape(rows // 2, 2, cols), ("chip", "core", "col"))
-    split = ("chip", "core")
-    placed = (P(split, "col", None, None), P(split, "col", None, None), P(None, "col"))
+    fine = Mesh(mesh.devices.reshape(rows // 4, 2, 2, cols), ROW + ("col",))
+    placed = (P(ROW, "col", None, None), P(ROW, "col", None, None), P(None, "col"))
     return jax.shard_map(
-        per_device, mesh=fine, in_specs=placed, out_specs=P(split, "col", None), check_vma=False
+        per_device, mesh=fine, in_specs=placed, out_specs=P(ROW, "col", None), check_vma=False
     )

time: 147 us -> 142 us (0.966); the launches traced: 147 us -> 140 us
  blocking collectives: 118 us -> 46.9 us
  waiting for transfers between devices: 0.01 us -> 32.1 us
  starting transfers between devices: 0.4 us -> 23.5 us
  local copies, waits for them, and re-layouts: 0.01 us -> 6.84 us
  Pallas kernels: 28 us -> 29.9 us
    all_to_all x4 -> x2, blocking collectives: 118 us -> 46.9 us  [the longest x1 29.5 us: across(): lax.all_to_all(x, ('z_lo', 'col'), 0, 0, axis_index_groups=groups, tiled=...]
    ppermute x0 -> x7, waiting for transfers between devices: none -> 23.9 us  [per_device(): pieces.append(lax.ppermute(message, CHIP, pairs))]
    all_to_all x0 -> x2, starting transfers between devices: none -> 14.4 us  [the longest x1 7.34 us: per_device(): got_query = lax.all_to_all(query_message, ROW, 0, 0, tiled=True)]
    ppermute x0 -> x7, starting transfers between devices: none -> 8.36 us  [per_device(): pieces.append(lax.ppermute(message, CHIP, pairs))]
    unnamed x2 -> x22, local copies, waits for them, and re-layouts: 0.01 us -> 6.84 us
    all_to_all x0 -> x2, waiting for transfers between devices: none -> 5.05 us  [the longest x1 5.04 us: per_device(): got_query = lax.all_to_all(query_message, ROW, 0, 0, tiled=True)]
    ppermute x1, waiting for transfers between devices: 0.01 us -> 3.13 us  [per_device(): other = lax.ppermute(own, 'core', [(0, 1), (1, 0)])]
    pallas_call x1 -> x3, Pallas kernels: 4.94 us -> 6.41 us  [the longest x1 4.08 us: pack(): pl.pallas_call(pack_kernel, grid=(chips // 2,), in_specs=[smem(), pl.Bloc...]
  transfers between devices with their start and end apart: 1 -> 10, of which waited for: 0 -> 8; matrix products, arithmetic and copies ran while one was open for 0% -> 0% of each run, Pallas kernels for 1% -> 3%
where the time goes in v4:
time: 142 us; the launch traced here: 140 us
  blocking collectives  46.9 us (33%)
  waiting for transfers between devices  32.1 us (23%)
  Pallas kernels  29.9 us (21%)
  starting transfers between devices  23.5 us (17%)
  local copies, waits for them, and re-layouts  6.84 us (5%)
    all_to_all x1, blocking collectives, across(): lax.all_to_all(x, ('z_lo', 'col'), 0, 0, axis_index_groups=groups, tiled=...  29.5 us
    ppermute x7, waiting for transfers between devices, per_device(): pieces.append(lax.ppermute(message, CHIP, pairs))  23.9 us
    pallas_call x1, Pallas kernels, attend(): pl.pallas_call(attend_kernel, in_specs=[smem(), vmem(), vmem(), vmem(), v...  17.5 us
    all_to_all x1, blocking collectives, per_device(): finished = lax.all_to_all(finished, ROW, 0, 0, tiled=True)  17.4 us
    ppermute x7, starting transfers between devices, per_device(): pieces.append(lax.ppermute(message, CHIP, pairs))  8.36 us
    all_to_all x1, starting transfers between devices, per_device(): got_query = lax.all_to_all(query_message, ROW, 0, 0, tiled=True)  7.34 us
    all_to_all x1, starting transfers between devices, across(): lax.all_to_all(x, ('z_lo', 'col'), 0, 0, axis_index_groups=groups, tiled=...  7.03 us
    unnamed x22, local copies, waits for them, and re-layouts  6.84 us
  transfers between devices with their start and end apart: 10, of which 8 were waited for; matrix products, arithmetic and copies ran while one was open for 0% of the time, Pallas kernels for 3%

profile of v4, /device:TPU:1, one launch (start us, length us, event | category | flops | bytes accessed | tf_op | source)
XLA Modules:
  0.0 139.9 jit_solution(16478672393890252391)
XLA Ops:
  0.0 2.1 %shard_map.37 = bf16[8,2,192,128]{3,2,1,0:T(8,128)(2,1)} custom-call(bf16[16,3,16,1536]{3,2,1,0:T(8,128)(2,1)} %bitcast.7), custom_call_target="tpu_custom_call" | custom-call | bytes 1572864 | tf_op jit(solution)/shard_map/pallas_call | solution.py:68
  2.1 7.3 %all-to-all-start = ((bf16[16,192,128]{2,1,0:T(8,128)(2,1)}), bf16[16,192,128]{2,1,0:T(8,128)(2,1)S(1)}, u32[]{:S(2)}, u32[]{:S(2)}) async-start(bf16[16,192,128]{2,1,0:T(8,128)(2,1)} %bitcast.17), calls=%async_computation | async-start | bytes 1572864 | tf_op jit(solution)/shard_map/all_to_all | solution.py:383
  9.5 1.4 %copy-done.1 = bf16[16,16,2,1536]{3,2,1,0:T(2,128)(2,1)S(1)} copy-done((bf16[16,16,2,1536]{3,2,1,0:T(2,128)(2,1)S(1)}, bf16[16,16,2,1536]{3,2,1,0:T(2,128)(2,1)}, u32[]{:S(2)}) %copy-start.1) | copy-done | bytes 1572888
  10.9 4.1 %shard_map.38 = (bf16[1024,128]{1,0:T(8,128)(2,1)S(1)}, bf16[1024,128]{1,0:T(8,128)(2,1)}, bf16[1024,128]{1,0:T(8,128)(2,1)}, bf16[1024,128]{1,0:T(8,128)(2,1)},...) custom-call(s32[4]{0:T(128)S(1)} %bitcast.13, ...), custom_call_target="tpu_custom_call" | custom-call | bytes 5505024 | tf_op jit(solution)/shard_map/pallas_call | solution.py:132
  15.0 0.7 copy-done.7
  15.7 0.7 copy-done.9
  16.4 0.7 copy-done.10
  17.1 5.0 %all-to-all-done.got_ref = bf16[16,192,128]{2,1,0:T(8,128)(2,1)S(1)} async-done(((bf16[16,192,128]{2,1,0:T(8,128)(2,1)}), bf16[16,192,128]{2,1,0:T(8,128)(2,1)S(1)}, u32[]{:S(2)}, u32[]{:S(2)}) %all-to-all-start) | async-done | bytes 786464 | tf_op jit(solution)/shard_map/all_to_all | solution.py:383
  22.1 2.0 %shard_map.39 = bf16[8,4,208,128]{3,2,1,0:T(8,128)(2,1)} custom-call(s32[4]{0:T(128)S(1)} %bitcast.14, bf16[16,192,128]{2,1,0:T(8,128)(2,1)S(1)} %all-to-all-done.got_ref), custom_call_target="tpu_custom_call" | custom-call | bytes 3407872 | tf_op jit(solution)/shard_map/pallas_call | solution.py:184
  24.1 7.0 %all-to-all-start.1 = ((bf16[8,4,208,128]{3,2,1,0:T(8,128)(2,1)}), bf16[8,4,208,128]{3,2,1,0:T(8,128)(2,1)S(1)}, u32[]{:S(2)}, u32[]{:S(2)}) async-start(bf16[8,4,208,128]{3,2,1,0:T(8,128)(2,1)} %shard_map.39), calls=%async_computation.1 | async-start | bytes 3407872 | tf_op jit(solution)/shard_map/all_to_all | solution.py:46
  31.1 0.9 collective-permute-start
  32.0 1.6 %collective-permute-start.1 = (bf16[1024,128]{1,0:T(8,128)(2,1)}, bf16[1024,128]{1,0:T(8,128)(2,1)S(1)}, u32[]{:S(2)}, u32[]{:S(2)}) collective-permute-start(bf16[1024,128]{1,0:T(8,128)(2,1)} %get-tuple-element.43), channel_id=1, source_target_pairs={{0,64},{16,80},{32,96},{48,112},{64,0},{80,16},{96,32},{112,48},{1... | collective-permute-start | bytes 786440 | tf_op jit(solution)/shard_map/ppermute | solution.py:391
  33.6 1.3 collective-permute-start.2
  35.0 1.0 collective-permute-start.3
  36.0 0.9 collective-permute-start.4
  36.9 4.3 %collective-permute-done.refs_1_ = bf16[1024,128]{1,0:T(8,128)(2,1)S(1)} collective-permute-done((bf16[1024,128]{1,0:T(8,128)(2,1)}, bf16[1024,128]{1,0:T(8,128)(2,1)S(1)}, u32[]{:S(2)}, u32[]{:S(2)}) %collective-permute-start) | collective-permute-done | bytes 262176 | tf_op jit(solution)/shard_map/ppermute | solution.py:391
  41.2 3.3 %collective-permute-done.1.refs_2_ = bf16[1024,128]{1,0:T(8,128)(2,1)S(1)} collective-permute-done((bf16[1024,128]{1,0:T(8,128)(2,1)}, bf16[1024,128]{1,0:T(8,128)(2,1)S(1)}, u32[]{:S(2)}, u32[]{:S(2)}) %collective-permute-start.1) | collective-permute-done | bytes 262176 | tf_op jit(solution)/shard_map/ppermute | solution.py:391
  44.5 2.6 %collective-permute-start.6 = (bf16[1024,128]{1,0:T(8,128)(2,1)S(1)}, bf16[1024,128]{1,0:T(8,128)(2,1)S(1)}, u32[]{:S(2)}, u32[]{:S(2)}) collective-permute-start(bf16[1024,128]{1,0:T(8,128)(2,1)S(1)} %copy-done.8), channel_id=1, source_target_pairs={{0,16},{16,0},{32,48},{48,32},{64,80},{80,64},{96,112},{112,96},{1... | collective-permute-start | bytes 786440 | tf_op jit(solution)/shard_map/ppermute | solution.py:391
  47.1 8.0 %collective-permute-done.2.refs_3_ = bf16[1024,128]{1,0:T(8,128)(2,1)S(1)} collective-permute-done((bf16[1024,128]{1,0:T(8,128)(2,1)}, bf16[1024,128]{1,0:T(8,128)(2,1)S(1)}, u32[]{:S(2)}, u32[]{:S(2)}) %collective-permute-start.2) | collective-permute-done | bytes 262176 | tf_op jit(solution)/shard_map/ppermute | solution.py:391
  55.1 2.6 %collective-permute-done.4.refs_5_ = bf16[1024,128]{1,0:T(8,128)(2,1)S(1)} collective-permute-done((bf16[1024,128]{1,0:T(8,128)(2,1)}, bf16[1024,128]{1,0:T(8,128)(2,1)S(1)}, u32[]{:S(2)}, u32[]{:S(2)}) %collective-permute-start.4) | collective-permute-done | bytes 262176 | tf_op jit(solution)/shard_map/ppermute | solution.py:391
  58.0 0.7 copy-done.2
  58.7 5.4 %collective-permute-done.6.refs_7_ = bf16[1024,128]{1,0:T(8,128)(2,1)S(1)} collective-permute-done((bf16[1024,128]{1,0:T(8,128)(2,1)S(1)}, bf16[1024,128]{1,0:T(8,128)(2,1)S(1)}, u32[]{:S(2)}, u32[]{:S(2)}) %collective-permute-start.6) | collective-permute-done | bytes 262176 | tf_op jit(solution)/shard_map/ppermute | solution.py:391
  64.1 0.7 copy-done.4
  64.8 0.9 copy-done.3
  65.8 0.9 copy-done.5
  67.0 0.7 collective-permute-start.7
  68.4 3.1 %collective-permute-done.7.other_ref = bf16[8,1024,128]{2,1,0:T(8,128)(2,1)S(1)} collective-permute-done((bf16[8,1024,128]{2,1,0:T(8,128)(2,1)S(1)}, bf16[8,1024,128]{2,1,0:T(8,128)(2,1)S(1)}, u32[]{:S(2)}, u32[]{:S(2)}) %collective-permute-start.7) | collective-permute-done | bytes 2097184 | tf_op jit(solution)/shard_map/ppermute | solution.py:395
  72.1 17.5 %shard_map.42 = bf16[32,208,128]{2,1,0:T(8,128)(2,1)S(1)} custom-call(s32[32]{0:T(128)S(1)} %fusion.valid_ref, bf16[32,208,128]{2,1,0:T(8,128)(2,1)S(1)} %bitcast.11, bf16[8,1024,128]{2,1,0:T(8,128)(2,1)S(1)} %shard_map.40.own_ref, bf16[8,1024,128]{2,1,0:T(8,128)(2,1)S(1)} %collective-permute-done.7.other_ref, bf16[2,4096,256]{2,1,0:T(8,128)(2,1)S(1)} %shard_map.41.values_ref), custom_call_target="tpu_custom_call" | custom-call | flops 20000000000 | bytes 8388608 | tf_op jit(solution)/shard_map/pallas_call | solution.py:302
  89.7 29.5 %all_to_all.20.part_ref = bf16[8,4,208,128]{3,2,1,0:T(8,128)(2,1)S(1)} all-to-all(bf16[8,4,208,128]{3,2,1,0:T(8,128)(2,1)S(1)} %bitcast.12), channel_id=1, replica_groups={{0,1,2,3,20,21,22,23},{16,17,18,19,4,5,6,7},{8,9,10,11,28,29,30,31},{24..., dimensions={0} | all-to-all | bytes 3407872 | tf_op jit(solution)/shard_map/all_to_all | solution.py:46
  119.2 1.4 shard_map.43
  120.5 17.4 %all_to_all.21 = bf16[16,192,128]{2,1,0:T(8,128)(2,1)} all-to-all(bf16[16,192,128]{2,1,0:T(8,128)(2,1)S(1)} %shard_map.43), channel_id=1, replica_groups=mesh['y'=4,'z_lo'=2,'core'=2,'col'=8] {'y','z_lo','core'}, dimensions={0} | all-to-all | bytes 1572864 | tf_op jit(solution)/shard_map/all_to_all | solution.py:403
  137.9 1.9 %shard_map.44 = bf16[256,1536]{1,0:T(8,128)(2,1)} custom-call(bf16[8,2,192,128]{3,2,1,0:T(8,128)(2,1)} %bitcast.16), custom_call_target="tpu_custom_call" | custom-call | bytes 1572864 | tf_op jit(solution)/shard_map/pallas_call | solution.py:365
  (21 shorter events, 1.8 us)
Async XLA Ops:
  0.0 9.5 %copy-start = (bf16[16,16,3,1536]{3,1,2,0:T(8,128)(2,1)S(1)}, bf16[16,16,3,1536]{3,1,2,0:T(8,128)(2,1)}, u32[]{:S(2)}) copy-start(bf16[16,16,3,1536]{3,1,2,0:T(8,128)(2,1)} %param.4) | copy-start | bytes 7077892
  0.0 9.5 %copy-start.6 = (s32[4,1]{0,1:T(1,128)S(1)}, s32[4,1]{0,1:T(1,128)}, u32[]{:S(2)}) copy-start(s32[4,1]{0,1:T(1,128)} %param.5) | copy-start | bytes 52
  2.1 20.0 %all-to-all-start = ((bf16[16,192,128]{2,1,0:T(8,128)(2,1)}), bf16[16,192,128]{2,1,0:T(8,128)(2,1)S(1)}, u32[]{:S(2)}, u32[]{:S(2)}) async-start(bf16[16,192,128]{2,1,0:T(8,128)(2,1)} %bitcast.17), calls=%async_computation | async-start | bytes 1572864 | tf_op jit(solution)/shard_map/all_to_all | solution.py:383
  9.5 1.4 %copy-start.1 = (bf16[16,16,2,1536]{3,2,1,0:T(2,128)(2,1)S(1)}, bf16[16,16,2,1536]{3,2,1,0:T(2,128)(2,1)}, u32[]{:S(2)}) copy-start(bf16[16,16,2,1536]{3,2,1,0:T(2,128)(2,1)} %cache_ref.1) | copy-start | bytes 4718596
  15.0 0.7 copy-start.7
  15.7 0.7 copy-start.9
  16.4 0.7 copy-start.10
  24.1 20.4 %copy-start.8 = (bf16[1024,128]{1,0:T(8,128)(2,1)S(1)}, bf16[1024,128]{1,0:T(8,128)(2,1)}, u32[]{:S(2)}) copy-start(bf16[1024,128]{1,0:T(8,128)(2,1)} %copy-done.7) | copy-start | bytes 786436
  24.1 40.7 %all-to-all-start.1 = ((bf16[8,4,208,128]{3,2,1,0:T(8,128)(2,1)}), bf16[8,4,208,128]{3,2,1,0:T(8,128)(2,1)S(1)}, u32[]{:S(2)}, u32[]{:S(2)}) async-start(bf16[8,4,208,128]{3,2,1,0:T(8,128)(2,1)} %shard_map.39), calls=%async_computation.1 | async-start | bytes 3407872 | tf_op jit(solution)/shard_map/all_to_all | solution.py:46
  31.1 10.0 %collective-permute-start = (bf16[1024,128]{1,0:T(8,128)(2,1)}, bf16[1024,128]{1,0:T(8,128)(2,1)S(1)}, u32[]{:S(2)}, u32[]{:S(2)}) collective-permute-start(bf16[1024,128]{1,0:T(8,128)(2,1)} %get-tuple-element.42), channel_id=1, source_target_pairs={{0,80},{16,64},{32,112},{48,96},{64,16},{80,0},{96,48},{112,32},{1... | collective-permute-start | bytes 786440 | tf_op jit(solution)/shard_map/ppermute | solution.py:391
  32.0 12.5 %collective-permute-start.1 = (bf16[1024,128]{1,0:T(8,128)(2,1)}, bf16[1024,128]{1,0:T(8,128)(2,1)S(1)}, u32[]{:S(2)}, u32[]{:S(2)}) collective-permute-start(bf16[1024,128]{1,0:T(8,128)(2,1)} %get-tuple-element.43), channel_id=1, source_target_pairs={{0,64},{16,80},{32,96},{48,112},{64,0},{80,16},{96,32},{112,48},{1... | collective-permute-start | bytes 786440 | tf_op jit(solution)/shard_map/ppermute | solution.py:391
  33.6 21.4 %collective-permute-start.2 = (bf16[1024,128]{1,0:T(8,128)(2,1)}, bf16[1024,128]{1,0:T(8,128)(2,1)S(1)}, u32[]{:S(2)}, u32[]{:S(2)}) collective-permute-start(bf16[1024,128]{1,0:T(8,128)(2,1)} %get-tuple-element.44), channel_id=1, source_target_pairs={{0,112},{16,96},{32,80},{48,64},{64,48},{80,32},{96,16},{112,0},{1... | collective-permute-start | bytes 786440 | tf_op jit(solution)/shard_map/ppermute | solution.py:391
  35.0 20.1 %collective-permute-start.3 = (bf16[1024,128]{1,0:T(8,128)(2,1)}, bf16[1024,128]{1,0:T(8,128)(2,1)S(1)}, u32[]{:S(2)}, u32[]{:S(2)}) collective-permute-start(bf16[1024,128]{1,0:T(8,128)(2,1)} %get-tuple-element.45), channel_id=1, source_target_pairs={{0,32},{16,48},{32,0},{48,16},{64,96},{80,112},{96,64},{112,80},{1... | collective-permute-start | bytes 786440 | tf_op jit(solution)/shard_map/ppermute | solution.py:391
  36.0 21.7 %collective-permute-start.4 = (bf16[1024,128]{1,0:T(8,128)(2,1)}, bf16[1024,128]{1,0:T(8,128)(2,1)S(1)}, u32[]{:S(2)}, u32[]{:S(2)}) collective-permute-start(bf16[1024,128]{1,0:T(8,128)(2,1)} %copy-done.10), channel_id=1, source_target_pairs={{0,48},{16,32},{32,16},{48,0},{64,112},{80,96},{96,80},{112,64},{1... | collective-permute-start | bytes 786440 | tf_op jit(solution)/shard_map/ppermute | solution.py:391
  41.2 16.8 %collective-permute-start.5 = (bf16[1024,128]{1,0:T(8,128)(2,1)}, bf16[1024,128]{1,0:T(8,128)(2,1)S(1)}, u32[]{:S(2)}, u32[]{:S(2)}) collective-permute-start(bf16[1024,128]{1,0:T(8,128)(2,1)} %copy-done.9), channel_id=1, source_target_pairs={{0,96},{16,112},{32,64},{48,80},{64,32},{80,48},{96,0},{112,16},{1... | collective-permute-start | bytes 786440 | tf_op jit(solution)/shard_map/ppermute | solution.py:391
  44.5 19.6 %collective-permute-start.6 = (bf16[1024,128]{1,0:T(8,128)(2,1)S(1)}, bf16[1024,128]{1,0:T(8,128)(2,1)S(1)}, u32[]{:S(2)}, u32[]{:S(2)}) collective-permute-start(bf16[1024,128]{1,0:T(8,128)(2,1)S(1)} %copy-done.8), channel_id=1, source_target_pairs={{0,16},{16,0},{32,48},{48,32},{64,80},{80,64},{96,112},{112,96},{1... | collective-permute-start | bytes 786440 | tf_op jit(solution)/shard_map/ppermute | solution.py:391
  58.0 0.7 copy-start.2
  64.1 0.7 copy-start.4
  64.8 1.0 copy-start.3
  65.8 0.9 copy-start.5
  67.0 4.5 %collective-permute-start.7 = (bf16[8,1024,128]{2,1,0:T(8,128)(2,1)S(1)}, bf16[8,1024,128]{2,1,0:T(8,128)(2,1)S(1)}, u32[]{:S(2)}, u32[]{:S(2)}) collective-permute-start(bf16[8,1024,128]{2,1,0:T(8,128)(2,1)S(1)} %shard_map.40.own_ref), channel_id=1, source_target_pairs={{0,8},{8,0},{1,9},{9,1},{2,10},{10,2},{3,11},{11,3},{4,12},{12,4},... | collective-permute-start | bytes 6291464 | tf_op jit(solution)/shard_map/ppermute | solution.py:395

commit v5 on v4

--- a/solution.py
+++ b/solution.py
@@ -12,7 +12,7 @@
 TOKS = 256
 HALF = 128
 QUART = 64
-KV_ROWS = 4 * TOKS
+KV_ROWS = 4 * HALF
 Q_ROWS = HALF + QUART
 SLOT_ROWS = Q_ROWS + 16
 GROUP = 4
@@ -32,11 +32,15 @@
 ROW = CHIP + ("core",)
 
 
-STEPS = (5, 4, 7, 2, 3, 6, 1)
-
-
 def flip():
     return lax.axis_index("col") // (lax.axis_size("col") // 2)
+
+
+def shift(x, step):
+    cols = lax.axis_size("col")
+    far = step // (cols // 2)
+    pairs = [(i, i ^ (far * cols + step)) for i in range(2 * cols)]
+    return lax.ppermute(x, ("z_lo", "col"), pairs)
 
 
 def across(x):
@@ -80,11 +84,8 @@
     return pl.BlockSpec((16, 1, 16, 3 * DEPTH), lambda p: (0, part, 0, p))
 
 
-def pack_kernel(rows_ref, cache_ref, keys_ref, values_ref, *refs):
-    out_refs, sorted_ref = refs[:-1], refs[-1]
-    my_chip = lax.axis_index(CHIP)
-    my_row = 2 * my_chip + lax.axis_index("core")
-    my_chip = jnp.bitwise_xor(my_chip, flip())
+def pack_kernel(rows_ref, cache_ref, keys_ref, values_ref, out_ref, sorted_ref):
+    my_row = lax.axis_index(ROW)
     edited = rows_ref[0] == my_row
     for slot in range(1, SLOTS):
         edited = jnp.logical_or(edited, rows_ref[slot] == my_row)
@@ -109,37 +110,29 @@
                     part * HALF : (part + 1) * HALF
                 ]
 
-    pair = jnp.bitwise_xor(pl.program_id(0), my_chip // 2)
-    swapped = jnp.bitwise_and(my_chip, 1)
-    for j in range(len(out_refs) // 2):
-        for i in range(2):
-            second = jnp.bitwise_xor(swapped, i)
-
-            for which in range(2):
-
-                @pl.when(jnp.logical_and(pair == j, second == which))
-                def _():
-                    full = slice(2 * which * DEPTH, (2 * which + 1) * DEPTH)
-                    out_ref = out_refs[((0,) + STEPS).index(2 * j + i)]
-                    for part in range(2):
-                        out_ref[part * TOKS : (part + 1) * TOKS, :] = sorted_ref[part, :, full]
-                        out_ref[(2 + part) * TOKS : (3 + part) * TOKS, :] = sorted_ref[
-                            part, :, DEPTH : 2 * DEPTH
-                        ]
-
-
-def pack(listed_rows, cache, fresh, chips):
+    for chip in range(2):
+        dest = jnp.bitwise_xor(chip, flip())
+        for core in range(2):
+            toks = slice(core * HALF, (core + 1) * HALF)
+            for i, head in enumerate((2 * chip, 1)):
+                cols = slice(head * DEPTH, (head + 1) * DEPTH)
+                for part in range(2):
+                    first = (2 * i + part) * HALF
+                    out_ref[2 * dest + core, first : first + HALF, :] = sorted_ref[part, toks, cols]
+
+
+def pack(listed_rows, cache, fresh):
     return pl.pallas_call(
         pack_kernel,
-        grid=(chips // 2,),
+        grid=(4,),
         in_specs=[
             smem(),
             pl.BlockSpec((16, 16, 2, 3 * DEPTH), lambda p: (0, 0, 0, p)),
             fresh_spec(1),
             fresh_spec(2),
         ],
-        out_specs=[vmem()] * chips,
-        out_shape=[jax.ShapeDtypeStruct((KV_ROWS, DEPTH), jnp.bfloat16)] * chips,
+        out_specs=pl.BlockSpec((4, KV_ROWS, DEPTH), lambda p: (p, 0, 0)),
+        out_shape=jax.ShapeDtypeStruct((16, KV_ROWS, DEPTH), jnp.bfloat16),
         scratch_shapes=[pltpu.VMEM((2, TOKS, 3 * DEPTH), jnp.bfloat16)],
         cost_estimate=cost(0, 7 * 786432),
         compiler_params=pltpu.CompilerParams(vmem_limit_bytes=20 * MIB),
@@ -161,7 +154,7 @@
         join_kernel,
         in_specs=[pl.BlockSpec(memory_space=pl.ANY)] * len(pieces),
         out_specs=vmem(),
-        out_shape=jax.ShapeDtypeStruct((len(pieces), KV_ROWS, DEPTH), jnp.bfloat16),
+        out_shape=jax.ShapeDtypeStruct((len(pieces),) + pieces[0].shape, jnp.bfloat16),
         scratch_shapes=[pltpu.SemaphoreType.DMA((len(pieces),))],
         cost_estimate=cost(0, 4 * MIB),
         compiler_params=pltpu.CompilerParams(vmem_limit_bytes=16 * MIB),
@@ -175,28 +168,27 @@
         rows = got_ref[jnp.minimum(row, bands - 1)]
         flag = jnp.where(row < bands, 1.0, 0.0)
         flags = jnp.full((SLOT_ROWS - Q_ROWS, DEPTH), flag, jnp.float32).astype(jnp.bfloat16)
-        for dest in range(out_ref.shape[0]):
-            out_ref[dest, slot, 0:Q_ROWS, :] = rows
-            out_ref[dest, slot, Q_ROWS:SLOT_ROWS, :] = flags
-
-
-def pick(listed_rows, received, copies):
+        out_ref[slot, 0:Q_ROWS, :] = rows
+        out_ref[slot, Q_ROWS:SLOT_ROWS, :] = flags
+
+
+def pick(listed_rows, received):
     return pl.pallas_call(
         pick_kernel,
         in_specs=[smem(), vmem()],
         out_specs=vmem(),
-        out_shape=jax.ShapeDtypeStruct((copies, SLOTS, SLOT_ROWS, DEPTH), jnp.bfloat16),
-        cost_estimate=cost(0, 2 * 1703936),
+        out_shape=jax.ShapeDtypeStruct((SLOTS, SLOT_ROWS, DEPTH), jnp.bfloat16),
+        cost_estimate=cost(0, 2 * 212992),
         compiler_params=pltpu.CompilerParams(vmem_limit_bytes=16 * MIB),
     )(listed_rows, received)
 
 
 def widen_kernel(own_ref, other_ref, out_ref):
     for head in range(2):
-        first = 2 * TOKS * head + TOKS
+        first = 2 * HALF * head + HALF
         for part, kv_ref in enumerate((own_ref, other_ref)):
             rows = slice(part * 2048, (part + 1) * 2048)
-            out_ref[head, rows, 0:DEPTH] = kv_ref[:, first : first + TOKS, :].reshape(2048, DEPTH)
+            out_ref[head, rows, 0:DEPTH] = kv_ref[:, first : first + HALF, :].reshape(2048, DEPTH)
         out_ref[head, :, DEPTH:] = jnp.ones((4096, DEPTH), jnp.bfloat16)
 
 
@@ -214,12 +206,12 @@
 def attend_rows(queries, kv_refs, values_ref, head):
     fold = math.log2(math.e) / math.sqrt(DEPTH)
     row_max = acc = None
-    tiles = KEY_BLOCK // TOKS
-    first = 2 * TOKS * head
+    tiles = KEY_BLOCK // HALF
+    first = 2 * HALF * head
     for part, kv_ref in enumerate(kv_refs):
         for block in range(kv_ref.shape[0] // tiles):
             rows = slice(block * tiles, (block + 1) * tiles)
-            keys = kv_ref[rows, first : first + TOKS, :].reshape(KEY_BLOCK, DEPTH)
+            keys = kv_ref[rows, first : first + HALF, :].reshape(KEY_BLOCK, DEPTH)
             scores = lax.dot_general(
                 queries, keys, (((1,), (1,)), ((), ())), preferred_element_type=jnp.float32
             )
@@ -267,6 +259,7 @@
         shared = jnp.concatenate([q_ref[pick, HALF:Q_ROWS, :] for pick in picks], axis=0)
         out_shared, lse_shared = attend_rows(shared, kv_refs, values_ref, 1)
         row_ids = lax.broadcasted_iota(jnp.int32, (16, DEPTH), 0)
+        picks = [jnp.bitwise_xor(pick, SLOTS * lax.axis_index("col")) for pick in picks]
         for i, pick in enumerate(picks):
             out_ref[pick, 0:HALF, :] = out_full[i * HALF : (i + 1) * HALF]
             out_ref[pick, HALF:Q_ROWS, :] = out_shared[i * QUART : (i + 1) * QUART]
@@ -382,16 +375,13 @@
     query_message = pack_query(fresh, chips)
     got_query = lax.all_to_all(query_message, ROW, 0, 0, tiled=True)
     fresh, query_message = lax.optimization_barrier((fresh, query_message))
-    messages = pack(listed_rows, kv_cache, fresh, chips)
-    spread = pick(listed_rows, got_query, col_count)
-    messages, spread = lax.optimization_barrier((messages, spread))
-    pieces = [messages[0]]
-    for step, message in zip(STEPS, messages[1:]):
-        pairs = [(i, i ^ step) for i in range(chips)]
-        pieces.append(lax.ppermute(message, CHIP, pairs))
-    queries = across(spread)
-    pieces, queries = lax.optimization_barrier((pieces, queries))
-    own = join(pieces)
+    message = pack(listed_rows, kv_cache, fresh)
+    picked = pick(listed_rows, got_query)
+    message, picked = lax.optimization_barrier((message, picked))
+    own = lax.all_to_all(message, ROW, 0, 0, tiled=True)
+    pieces = [picked] + [shift(picked, step) for step in range(1, col_count)]
+    pieces, own = lax.optimization_barrier((pieces, own))
+    queries = join(pieces)
     other = lax.ppermute(own, "core", [(0, 1), (1, 0)])
     queries = queries.reshape(col_count * SLOTS, SLOT_ROWS, DEPTH)
     valid = queries[:, Q_ROWS, 0].astype(jnp.int32)

time: 142 us -> 133 us (0.937); the launches traced: 140 us -> 134 us
  waiting for transfers between devices: 32.1 us -> 24.3 us
  blocking collectives: 46.9 us -> 48.6 us
    ppermute x7, waiting for transfers between devices: 23.9 us -> 17.1 us  [shift(): return lax.ppermute(x, ('z_lo', 'col'), pairs)]
    ppermute x1, waiting for transfers between devices: 3.13 us -> 0.01 us  [per_device(): other = lax.ppermute(own, 'core', [(0, 1), (1, 0)])]
    ppermute x7, starting transfers between devices: 8.36 us -> 11.1 us  [shift(): return lax.ppermute(x, ('z_lo', 'col'), pairs)]
    all_to_all x1, starting transfers between devices: 7.03 us -> 4.63 us  [per_device(): own = lax.all_to_all(message, ROW, 0, 0, tiled=True)]
    all_to_all x1, waiting for transfers between devices: 5.04 us -> 7.15 us  [per_device(): got_query = lax.all_to_all(query_message, ROW, 0, 0, tiled=True)]
    pallas_call x1, Pallas kernels: 0.23 us -> 2.24 us  [join(): pl.pallas_call(join_kernel, in_specs=[pl.BlockSpec(memory_space=pl.ANY)]...]
    pallas_call x1, Pallas kernels: 1.99 us -> 0.56 us  [pick(): pl.pallas_call(pick_kernel, in_specs=[smem(), vmem()], out_specs=vmem(),...]
    unnamed x22 -> x16, local copies, waits for them, and re-layouts: 6.84 us -> 5.98 us
  transfers between devices with their start and end apart: 10 -> 10, of which waited for: 8 -> 7; matrix products, arithmetic and copies ran while one was open for 0% -> 0% of each run, Pallas kernels for 3% -> 4%
where the time goes in v5:
time: 133 us; the launch traced here: 134 us
  blocking collectives  48.6 us (37%)
  Pallas kernels  29.7 us (22%)
  waiting for transfers between devices  24.3 us (18%)
  starting transfers between devices  24.2 us (18%)
  local copies, waits for them, and re-layouts  5.98 us (4%)
    all_to_all x1, blocking collectives, across(): lax.all_to_all(x, ('z_lo', 'col'), 0, 0, axis_index_groups=groups, tiled=...  30.4 us
    pallas_call x1, Pallas kernels, attend(): pl.pallas_call(attend_kernel, in_specs=[smem(), vmem(), vmem(), vmem(), v...  18.5 us
    all_to_all x1, blocking collectives, per_device(): finished = lax.all_to_all(finished, ROW, 0, 0, tiled=True)  18.3 us
    ppermute x7, waiting for transfers between devices, shift(): return lax.ppermute(x, ('z_lo', 'col'), pairs)  17.1 us
    ppermute x7, starting transfers between devices, shift(): return lax.ppermute(x, ('z_lo', 'col'), pairs)  11.1 us
    all_to_all x1, starting transfers between devices, per_device(): got_query = lax.all_to_all(query_message, ROW, 0, 0, tiled=True)  7.34 us
    all_to_all x1, waiting for transfers between devices, per_device(): got_query = lax.all_to_all(query_message, ROW, 0, 0, tiled=True)  7.15 us
    unnamed x16, local copies, waits for them, and re-layouts  5.98 us
  transfers between devices with their start and end apart: 10, of which 7 were waited for; matrix products, arithmetic and copies ran while one was open for 0% of the time, Pallas kernels for 4%

profile of v5, /device:TPU:1, one launch (start us, length us, event | category | flops | bytes accessed | tf_op | source)
XLA Modules:
  0.0 133.6 jit_solution(9838073648829701476)
XLA Ops:
  0.0 2.1 %shard_map.37 = bf16[8,2,192,128]{3,2,1,0:T(8,128)(2,1)} custom-call(bf16[16,3,16,1536]{3,2,1,0:T(8,128)(2,1)} %bitcast.7), custom_call_target="tpu_custom_call" | custom-call | bytes 1572864 | tf_op jit(solution)/shard_map/pallas_call | solution.py:72
  2.1 7.3 %all-to-all-start = ((bf16[16,192,128]{2,1,0:T(8,128)(2,1)}), bf16[16,192,128]{2,1,0:T(8,128)(2,1)S(1)}, u32[]{:S(2)}, u32[]{:S(2)}) async-start(bf16[16,192,128]{2,1,0:T(8,128)(2,1)} %bitcast.17), calls=%async_computation | async-start | bytes 1572864 | tf_op jit(solution)/shard_map/all_to_all | solution.py:376
  9.5 1.4 %copy-done.2 = bf16[16,16,2,1536]{3,2,1,0:T(2,128)(2,1)S(1)} copy-done((bf16[16,16,2,1536]{3,2,1,0:T(2,128)(2,1)S(1)}, bf16[16,16,2,1536]{3,2,1,0:T(2,128)(2,1)}, u32[]{:S(2)}) %copy-start.2) | copy-done | bytes 1572888
  10.9 2.7 %shard_map.38 = bf16[16,512,128]{2,1,0:T(8,128)(2,1)S(1)} custom-call(s32[4]{0:T(128)S(1)} %bitcast.13, bf16[16,16,2,1536]{3,2,1,0:T(2,128)(2,1)S(1)} %copy-done.2, bf16[16,3,16,1536]{3,2,1,0:T(8,128)(2,1)S(1)} %bitcast.8, bf16[16,3,16,1536]{3,2,1,0:T(8,128)(2,1)S(1)} %bitcast.9), custom_call_target="tpu_custom_call" | custom-call | bytes 5505024 | tf_op jit(solution)/shard_map/pallas_call | solution.py:125
  13.6 1.3 copy-done.1
  15.0 7.2 %all-to-all-done.got_ref = bf16[16,192,128]{2,1,0:T(8,128)(2,1)S(1)} async-done(((bf16[16,192,128]{2,1,0:T(8,128)(2,1)}), bf16[16,192,128]{2,1,0:T(8,128)(2,1)S(1)}, u32[]{:S(2)}, u32[]{:S(2)}) %all-to-all-start) | async-done | bytes 786464 | tf_op jit(solution)/shard_map/all_to_all | solution.py:376
  22.1 0.6 shard_map.39.refs_0_
  22.7 4.6 %all-to-all-start.1 = ((bf16[16,512,128]{2,1,0:T(8,128)(2,1)}), bf16[16,512,128]{2,1,0:T(8,128)(2,1)S(1)}, u32[]{:S(2)}, u32[]{:S(2)}) async-start(bf16[16,512,128]{2,1,0:T(8,128)(2,1)} %copy-done.1), calls=%async_computation.1 | async-start | bytes 4194304 | tf_op jit(solution)/shard_map/all_to_all | solution.py:381
  27.3 5.7 %collective-permute-start.6 = (bf16[4,208,128]{2,1,0:T(8,128)(2,1)S(1)}, bf16[4,208,128]{2,1,0:T(8,128)(2,1)S(1)}, u32[]{:S(2)}, u32[]{:S(2)}) collective-permute-start(bf16[4,208,128]{2,1,0:T(8,128)(2,1)S(1)} %shard_map.39.refs_0_), channel_id=1, source_target_pairs={{0,23},{1,22},{2,21},{3,20},{4,19},{5,18},{6,17},{7,16},{16,7},{17... | collective-permute-start | bytes 638984 | tf_op jit(solution)/shard_map/ppermute | solution.py:43
  33.0 0.4 collective-permute-start.5
  33.4 2.5 %collective-permute-start.4 = (bf16[4,208,128]{2,1,0:T(8,128)(2,1)S(1)}, bf16[4,208,128]{2,1,0:T(8,128)(2,1)S(1)}, u32[]{:S(2)}, u32[]{:S(2)}) collective-permute-start(bf16[4,208,128]{2,1,0:T(8,128)(2,1)S(1)} %shard_map.39.refs_0_), channel_id=1, source_target_pairs={{0,21},{1,20},{2,23},{3,22},{4,17},{5,16},{6,19},{7,18},{16,5},{17... | collective-permute-start | bytes 638984 | tf_op jit(solution)/shard_map/ppermute | solution.py:43
  35.9 0.2 collective-permute-start.3
  36.1 2.3 %collective-permute-start.2 = (bf16[4,208,128]{2,1,0:T(8,128)(2,1)S(1)}, bf16[4,208,128]{2,1,0:T(8,128)(2,1)S(1)}, u32[]{:S(2)}, u32[]{:S(2)}) collective-permute-start(bf16[4,208,128]{2,1,0:T(8,128)(2,1)S(1)} %shard_map.39.refs_0_), channel_id=1, source_target_pairs={{0,3},{1,2},{2,1},{3,0},{4,7},{5,6},{6,5},{7,4},{16,19},{17,18},{1... | collective-permute-start | bytes 638984 | tf_op jit(solution)/shard_map/ppermute | solution.py:43
  38.4 5.8 %collective-permute-done.6.refs_7_ = bf16[4,208,128]{2,1,0:T(8,128)(2,1)S(1)} collective-permute-done((bf16[4,208,128]{2,1,0:T(8,128)(2,1)S(1)}, bf16[4,208,128]{2,1,0:T(8,128)(2,1)S(1)}, u32[]{:S(2)}, u32[]{:S(2)}) %collective-permute-start.6) | collective-permute-done | bytes 213024 | tf_op jit(solution)/shard_map/ppermute | solution.py:43
  44.2 3.2 %collective-permute-done.4.refs_5_ = bf16[4,208,128]{2,1,0:T(8,128)(2,1)S(1)} collective-permute-done((bf16[4,208,128]{2,1,0:T(8,128)(2,1)S(1)}, bf16[4,208,128]{2,1,0:T(8,128)(2,1)S(1)}, u32[]{:S(2)}, u32[]{:S(2)}) %collective-permute-start.4) | collective-permute-done | bytes 213024 | tf_op jit(solution)/shard_map/ppermute | solution.py:43
  47.4 5.5 %collective-permute-done.3.refs_4_ = bf16[4,208,128]{2,1,0:T(8,128)(2,1)S(1)} collective-permute-done((bf16[4,208,128]{2,1,0:T(8,128)(2,1)S(1)}, bf16[4,208,128]{2,1,0:T(8,128)(2,1)S(1)}, u32[]{:S(2)}, u32[]{:S(2)}) %collective-permute-start.3) | collective-permute-done | bytes 213024 | tf_op jit(solution)/shard_map/ppermute | solution.py:43
  52.9 0.2 collective-permute-done.2.refs_3_
  53.2 0.2 collective-permute-done.1.refs_2_
  53.4 0.7 copy-done.3
  54.1 2.1 %collective-permute-done.refs_1_ = bf16[4,208,128]{2,1,0:T(8,128)(2,1)S(1)} collective-permute-done((bf16[4,208,128]{2,1,0:T(8,128)(2,1)S(1)}, bf16[4,208,128]{2,1,0:T(8,128)(2,1)S(1)}, u32[]{:S(2)}, u32[]{:S(2)}) %collective-permute-start) | collective-permute-done | bytes 213024 | tf_op jit(solution)/shard_map/ppermute | solution.py:43
  56.2 0.7 copy-done.5
  56.9 1.2 collective-permute-start.7
  58.1 0.9 copy-done.4
  59.0 0.9 copy-done.6
  59.9 2.2 %shard_map.40 = bf16[8,4,208,128]{3,2,1,0:T(8,128)(2,1)S(1)} custom-call(bf16[4,208,128]{2,1,0:T(8,128)(2,1)S(1)} %shard_map.39.refs_0_, bf16[4,208,128]{2,1,0:T(8,128)(2,1)S(1)} %copy-done.6, bf16[4,208,128]{2,1,0:T(8,128)(2,1)S(1)} %copy-done.4, bf16[4,208,128]{2,1,0:T(8,128)(2,1)S(1)} %collective-permute-done.2.refs_3_, ...), custom_call_target="tpu_custom_call" | custom-call | bytes 4194304 | tf_op jit(solution)/shard_map/pallas_call | solution.py:153
  62.2 0.7 fusion.valid_ref
  62.9 0.6 shard_map.41.values_ref
  63.5 18.5 %shard_map.42 = bf16[32,208,128]{2,1,0:T(8,128)(2,1)S(1)} custom-call(s32[32]{0:T(128)S(1)} %fusion.valid_ref, bf16[32,208,128]{2,1,0:T(8,128)(2,1)S(1)} %bitcast.11, bf16[16,512,128]{2,1,0:T(8,128)(2,1)S(1)} %all-to-all-done.1.own_ref, bf16[16,512,128]{2,1,0:T(8,128)(2,1)S(1)} %collective-permute-done.7.other_ref, ...), custom_call_target="tpu_custom_call" | custom-call | flops 20000000000 | bytes 8388608 | tf_op jit(solution)/shard_map/pallas_call | solution.py:295
  82.0 30.4 %all_to_all.20.part_ref = bf16[8,4,208,128]{3,2,1,0:T(8,128)(2,1)S(1)} all-to-all(bf16[8,4,208,128]{3,2,1,0:T(8,128)(2,1)S(1)} %bitcast.12), channel_id=1, replica_groups={{0,1,2,3,20,21,22,23},{16,17,18,19,4,5,6,7},{8,9,10,11,28,29,30,31},{24..., dimensions={0} | all-to-all | bytes 3407872 | tf_op jit(solution)/shard_map/all_to_all | solution.py:50
  112.3 1.0 shard_map.43
  113.4 18.3 %all_to_all.21 = bf16[16,192,128]{2,1,0:T(8,128)(2,1)} all-to-all(bf16[16,192,128]{2,1,0:T(8,128)(2,1)S(1)} %shard_map.43), channel_id=1, replica_groups=mesh['y'=4,'z_lo'=2,'core'=2,'col'=8] {'y','z_lo','core'}, dimensions={0} | all-to-all | bytes 1572864 | tf_op jit(solution)/shard_map/all_to_all | solution.py:393
  131.6 1.9 %shard_map.44 = bf16[256,1536]{1,0:T(8,128)(2,1)} custom-call(bf16[8,2,192,128]{3,2,1,0:T(8,128)(2,1)} %bitcast.16), custom_call_target="tpu_custom_call" | custom-call | bytes 1572864 | tf_op jit(solution)/shard_map/pallas_call | solution.py:358
  (15 shorter events, 0.0 us)
Async XLA Ops:
  0.0 9.5 %copy-start = (bf16[16,16,3,1536]{3,1,2,0:T(8,128)(2,1)S(1)}, bf16[16,16,3,1536]{3,1,2,0:T(8,128)(2,1)}, u32[]{:S(2)}) copy-start(bf16[16,16,3,1536]{3,1,2,0:T(8,128)(2,1)} %param.4) | copy-start | bytes 7077892
  0.0 9.5 %copy-start.7 = (s32[4,1]{0,1:T(1,128)S(1)}, s32[4,1]{0,1:T(1,128)}, u32[]{:S(2)}) copy-start(s32[4,1]{0,1:T(1,128)} %param.5) | copy-start | bytes 52
  2.1 20.0 %all-to-all-start = ((bf16[16,192,128]{2,1,0:T(8,128)(2,1)}), bf16[16,192,128]{2,1,0:T(8,128)(2,1)S(1)}, u32[]{:S(2)}, u32[]{:S(2)}) async-start(bf16[16,192,128]{2,1,0:T(8,128)(2,1)} %bitcast.17), calls=%async_computation | async-start | bytes 1572864 | tf_op jit(solution)/shard_map/all_to_all | solution.py:376
  9.5 1.4 %copy-start.2 = (bf16[16,16,2,1536]{3,2,1,0:T(2,128)(2,1)S(1)}, bf16[16,16,2,1536]{3,2,1,0:T(2,128)(2,1)}, u32[]{:S(2)}) copy-start(bf16[16,16,2,1536]{3,2,1,0:T(2,128)(2,1)} %cache_ref.1) | copy-start | bytes 4718596
  13.6 1.3 %copy-start.1 = (bf16[16,512,128]{2,1,0:T(8,128)(2,1)}, bf16[16,512,128]{2,1,0:T(8,128)(2,1)S(1)}, u32[]{:S(2)}) copy-start(bf16[16,512,128]{2,1,0:T(8,128)(2,1)S(1)} %shard_map.38) | copy-start | bytes 6291460
  22.7 34.2 %all-to-all-start.1 = ((bf16[16,512,128]{2,1,0:T(8,128)(2,1)}), bf16[16,512,128]{2,1,0:T(8,128)(2,1)S(1)}, u32[]{:S(2)}, u32[]{:S(2)}) async-start(bf16[16,512,128]{2,1,0:T(8,128)(2,1)} %copy-done.1), calls=%async_computation.1 | async-start | bytes 4194304 | tf_op jit(solution)/shard_map/all_to_all | solution.py:381
  27.3 16.9 %collective-permute-start.6 = (bf16[4,208,128]{2,1,0:T(8,128)(2,1)S(1)}, bf16[4,208,128]{2,1,0:T(8,128)(2,1)S(1)}, u32[]{:S(2)}, u32[]{:S(2)}) collective-permute-start(bf16[4,208,128]{2,1,0:T(8,128)(2,1)S(1)} %shard_map.39.refs_0_), channel_id=1, source_target_pairs={{0,23},{1,22},{2,21},{3,20},{4,19},{5,18},{6,17},{7,16},{16,7},{17... | collective-permute-start | bytes 638984 | tf_op jit(solution)/shard_map/ppermute | solution.py:43
  33.0 11.2 %collective-permute-start.5 = (bf16[4,208,128]{2,1,0:T(8,128)(2,1)S(1)}, bf16[4,208,128]{2,1,0:T(8,128)(2,1)S(1)}, u32[]{:S(2)}, u32[]{:S(2)}) collective-permute-start(bf16[4,208,128]{2,1,0:T(8,128)(2,1)S(1)} %shard_map.39.refs_0_), channel_id=1, source_target_pairs={{0,22},{1,23},{2,20},{3,21},{4,18},{5,19},{6,16},{7,17},{16,6},{17... | collective-permute-start | bytes 638984 | tf_op jit(solution)/shard_map/ppermute | solution.py:43
  33.4 14.1 %collective-permute-start.4 = (bf16[4,208,128]{2,1,0:T(8,128)(2,1)S(1)}, bf16[4,208,128]{2,1,0:T(8,128)(2,1)S(1)}, u32[]{:S(2)}, u32[]{:S(2)}) collective-permute-start(bf16[4,208,128]{2,1,0:T(8,128)(2,1)S(1)} %shard_map.39.refs_0_), channel_id=1, source_target_pairs={{0,21},{1,20},{2,23},{3,22},{4,17},{5,16},{6,19},{7,18},{16,5},{17... | collective-permute-start | bytes 638984 | tf_op jit(solution)/shard_map/ppermute | solution.py:43
  35.9 17.0 %collective-permute-start.3 = (bf16[4,208,128]{2,1,0:T(8,128)(2,1)S(1)}, bf16[4,208,128]{2,1,0:T(8,128)(2,1)S(1)}, u32[]{:S(2)}, u32[]{:S(2)}) collective-permute-start(bf16[4,208,128]{2,1,0:T(8,128)(2,1)S(1)} %shard_map.39.refs_0_), channel_id=1, source_target_pairs={{0,20},{1,21},{2,22},{3,23},{4,16},{5,17},{6,18},{7,19},{16,4},{17... | collective-permute-start | bytes 638984 | tf_op jit(solution)/shard_map/ppermute | solution.py:43
  36.1 17.1 %collective-permute-start.2 = (bf16[4,208,128]{2,1,0:T(8,128)(2,1)S(1)}, bf16[4,208,128]{2,1,0:T(8,128)(2,1)S(1)}, u32[]{:S(2)}, u32[]{:S(2)}) collective-permute-start(bf16[4,208,128]{2,1,0:T(8,128)(2,1)S(1)} %shard_map.39.refs_0_), channel_id=1, source_target_pairs={{0,3},{1,2},{2,1},{3,0},{4,7},{5,6},{6,5},{7,4},{16,19},{17,18},{1... | collective-permute-start | bytes 638984 | tf_op jit(solution)/shard_map/ppermute | solution.py:43
  44.2 9.2 %collective-permute-start.1 = (bf16[4,208,128]{2,1,0:T(8,128)(2,1)S(1)}, bf16[4,208,128]{2,1,0:T(8,128)(2,1)S(1)}, u32[]{:S(2)}, u32[]{:S(2)}) collective-permute-start(bf16[4,208,128]{2,1,0:T(8,128)(2,1)S(1)} %shard_map.39.refs_0_), channel_id=1, source_target_pairs={{0,2},{1,3},{2,0},{3,1},{4,6},{5,7},{6,4},{7,5},{16,18},{17,19},{1... | collective-permute-start | bytes 638984 | tf_op jit(solution)/shard_map/ppermute | solution.py:43
  44.2 12.0 %collective-permute-start = (bf16[4,208,128]{2,1,0:T(8,128)(2,1)S(1)}, bf16[4,208,128]{2,1,0:T(8,128)(2,1)S(1)}, u32[]{:S(2)}, u32[]{:S(2)}) collective-permute-start(bf16[4,208,128]{2,1,0:T(8,128)(2,1)S(1)} %shard_map.39.refs_0_), channel_id=1, source_target_pairs={{0,1},{1,0},{2,3},{3,2},{4,5},{5,4},{6,7},{7,6},{16,17},{17,16},{1... | collective-permute-start | bytes 638984 | tf_op jit(solution)/shard_map/ppermute | solution.py:43
  53.4 0.7 copy-start.3
  56.2 0.7 copy-start.5
  56.9 6.0 %collective-permute-start.7 = (bf16[16,512,128]{2,1,0:T(8,128)(2,1)S(1)}, bf16[16,512,128]{2,1,0:T(8,128)(2,1)S(1)}, u32[]{:S(2)}, u32[]{:S(2)}) collective-permute-start(bf16[16,512,128]{2,1,0:T(8,128)(2,1)S(1)} %all-to-all-done.1.own_ref), channel_id=1, source_target_pairs={{0,8},{8,0},{1,9},{9,1},{2,10},{10,2},{3,11},{11,3},{4,12},{12,4},... | collective-permute-start | bytes 6291464 | tf_op jit(solution)/shard_map/ppermute | solution.py:385
  58.1 0.9 copy-start.4
  59.0 0.9 copy-start.6

commit v6 on v5

--- a/solution.py
+++ b/solution.py
@@ -15,7 +15,7 @@
 KV_ROWS = 4 * HALF
 Q_ROWS = HALF + QUART
 SLOT_ROWS = Q_ROWS + 16
-GROUP = 4
+GROUP = 8
 KEY_BLOCK = 512
 MIB = 1024 * 1024
 
@@ -140,24 +140,18 @@
 
 
 def join_kernel(*refs):
-    count = len(refs) - 2
-    out_ref, arrived = refs[count], refs[count + 1]
-    copies = [pltpu.make_async_copy(refs[i], out_ref.at[i], arrived.at[i]) for i in range(count)]
-    for copy in copies:
-        copy.start()
-    for copy in copies:
-        copy.wait()
+    for i, ref in enumerate(refs[:-1]):
+        refs[-1][i] = ref[...]
 
 
 def join(pieces):
     return pl.pallas_call(
         join_kernel,
-        in_specs=[pl.BlockSpec(memory_space=pl.ANY)] * len(pieces),
+        in_specs=[vmem()] * len(pieces),
         out_specs=vmem(),
         out_shape=jax.ShapeDtypeStruct((len(pieces),) + pieces[0].shape, jnp.bfloat16),
-        scratch_shapes=[pltpu.SemaphoreType.DMA((len(pieces),))],
         cost_estimate=cost(0, 4 * MIB),
-        compiler_params=pltpu.CompilerParams(vmem_limit_bytes=16 * MIB),
+        compiler_params=pltpu.CompilerParams(vmem_limit_bytes=8 * MIB),
     )(*pieces)
 
 
@@ -277,17 +271,23 @@
                     stats = jnp.where(row_ids == 3 * j + term, piece, stats)
             out_ref[pick, Q_ROWS:SLOT_ROWS, :] = stats.astype(jnp.bfloat16)
 
-    groups = (count + 1) // GROUP
+    eights = (count + 1) // GROUP
+    left = count - eights * GROUP
 
     def body(group, carry):
         attend_tiles(group * GROUP, GROUP)
         return carry
 
-    lax.fori_loop(0, groups, body, 0)
-
-    @pl.when(groups * GROUP < count)
+    lax.fori_loop(0, eights, body, 0)
+    fours = (left + 1) // 4
+
+    @pl.when(fours > 0)
     def _():
-        attend_tiles(groups * GROUP, 2)
+        attend_tiles(eights * GROUP, 4)
+
+    @pl.when(left > 4 * fours)
+    def _():
+        attend_tiles(eights * GROUP + 4 * fours, 2)
 
 
 def attend(valid, queries, own, other, values):

time: 133 us -> 132 us (level)
  Pallas kernels: 29.7 us -> 26.9 us
    pallas_call x1, Pallas kernels: 2.24 us -> 0.11 us  [join(): pl.pallas_call(join_kernel, in_specs=[vmem()] * len(pieces), out_specs=vm...]
  transfers between devices with their start and end apart: 10 -> 10, of which waited for: 7 -> 8; matrix products, arithmetic and copies ran while one was open for 0% -> 1% of each run, Pallas kernels for 4% -> 2%
where the time goes in v6:
time: 132 us
  blocking collectives  48.6 us (37%)
  Pallas kernels  26.9 us (20%)
  waiting for transfers between devices  25.4 us (19%)
  starting transfers between devices  24.2 us (18%)
  local copies, waits for them, and re-layouts  5.98 us (5%)
    all_to_all x1, blocking collectives, across(): lax.all_to_all(x, ('z_lo', 'col'), 0, 0, axis_index_groups=groups, tiled=...  30.3 us
    all_to_all x1, blocking collectives, per_device(): finished = lax.all_to_all(finished, ROW, 0, 0, tiled=True)  18.4 us
    pallas_call x1, Pallas kernels, attend(): pl.pallas_call(attend_kernel, in_specs=[smem(), vmem(), vmem(), vmem(), v...  17.8 us
    ppermute x7, waiting for transfers between devices, shift(): return lax.ppermute(x, ('z_lo', 'col'), pairs)  17.1 us
    ppermute x7, starting transfers between devices, shift(): return lax.ppermute(x, ('z_lo', 'col'), pairs)  11.1 us
    all_to_all x1, starting transfers between devices, per_device(): got_query = lax.all_to_all(query_message, ROW, 0, 0, tiled=True)  7.34 us
    all_to_all x1, waiting for transfers between devices, per_device(): got_query = lax.all_to_all(query_message, ROW, 0, 0, tiled=True)  7.15 us
    unnamed x16, local copies, waits for them, and re-layouts  5.98 us
  transfers between devices with their start and end apart: 10, of which 8 were waited for; matrix products, arithmetic and copies ran while one was open for 1% of the time, Pallas kernels for 2%

profile of v6, /device:TPU:1, one launch (start us, length us, event | category | flops | bytes accessed | tf_op | source)
XLA Modules:
  0.0 131.9 jit_solution(7128893759078105555)
XLA Ops:
  0.0 2.1 %shard_map.37 = bf16[8,2,192,128]{3,2,1,0:T(8,128)(2,1)} custom-call(bf16[16,3,16,1536]{3,2,1,0:T(8,128)(2,1)} %bitcast.7), custom_call_target="tpu_custom_call" | custom-call | bytes 1572864 | tf_op jit(solution)/shard_map/pallas_call | solution.py:72
  2.1 7.3 %all-to-all-start = ((bf16[16,192,128]{2,1,0:T(8,128)(2,1)}), bf16[16,192,128]{2,1,0:T(8,128)(2,1)S(1)}, u32[]{:S(2)}, u32[]{:S(2)}) async-start(bf16[16,192,128]{2,1,0:T(8,128)(2,1)} %bitcast.17), calls=%async_computation | async-start | bytes 1572864 | tf_op jit(solution)/shard_map/all_to_all | solution.py:376
  9.5 1.4 %copy-done.2 = bf16[16,16,2,1536]{3,2,1,0:T(2,128)(2,1)S(1)} copy-done((bf16[16,16,2,1536]{3,2,1,0:T(2,128)(2,1)S(1)}, bf16[16,16,2,1536]{3,2,1,0:T(2,128)(2,1)}, u32[]{:S(2)}) %copy-start.2) | copy-done | bytes 1572888
  10.9 2.7 %shard_map.38 = bf16[16,512,128]{2,1,0:T(8,128)(2,1)S(1)} custom-call(s32[4]{0:T(128)S(1)} %bitcast.13, bf16[16,16,2,1536]{3,2,1,0:T(2,128)(2,1)S(1)} %copy-done.2, bf16[16,3,16,1536]{3,2,1,0:T(8,128)(2,1)S(1)} %bitcast.8, bf16[16,3,16,1536]{3,2,1,0:T(8,128)(2,1)S(1)} %bitcast.9), custom_call_target="tpu_custom_call" | custom-call | bytes 5505024 | tf_op jit(solution)/shard_map/pallas_call | solution.py:125
  13.6 1.3 %copy-done.1 = bf16[16,512,128]{2,1,0:T(8,128)(2,1)} copy-done((bf16[16,512,128]{2,1,0:T(8,128)(2,1)}, bf16[16,512,128]{2,1,0:T(8,128)(2,1)S(1)}, u32[]{:S(2)}) %copy-start.1) | copy-done | bytes 2097176
  15.0 7.2 %all-to-all-done.got_ref = bf16[16,192,128]{2,1,0:T(8,128)(2,1)S(1)} async-done(((bf16[16,192,128]{2,1,0:T(8,128)(2,1)}), bf16[16,192,128]{2,1,0:T(8,128)(2,1)S(1)}, u32[]{:S(2)}, u32[]{:S(2)}) %all-to-all-start) | async-done | bytes 786464 | tf_op jit(solution)/shard_map/all_to_all | solution.py:376
  22.1 0.6 shard_map.39.refs_0_
  22.7 4.6 %all-to-all-start.1 = ((bf16[16,512,128]{2,1,0:T(8,128)(2,1)}), bf16[16,512,128]{2,1,0:T(8,128)(2,1)S(1)}, u32[]{:S(2)}, u32[]{:S(2)}) async-start(bf16[16,512,128]{2,1,0:T(8,128)(2,1)} %copy-done.1), calls=%async_computation.1 | async-start | bytes 4194304 | tf_op jit(solution)/shard_map/all_to_all | solution.py:381
  27.3 5.7 %collective-permute-start.6 = (bf16[4,208,128]{2,1,0:T(8,128)(2,1)S(1)}, bf16[4,208,128]{2,1,0:T(8,128)(2,1)S(1)}, u32[]{:S(2)}, u32[]{:S(2)}) collective-permute-start(bf16[4,208,128]{2,1,0:T(8,128)(2,1)S(1)} %shard_map.39.refs_0_), channel_id=1, source_target_pairs={{0,23},{1,22},{2,21},{3,20},{4,19},{5,18},{6,17},{7,16},{16,7},{17... | collective-permute-start | bytes 638984 | tf_op jit(solution)/shard_map/ppermute | solution.py:43
  33.0 0.4 collective-permute-start.5
  33.4 2.5 %collective-permute-start.4 = (bf16[4,208,128]{2,1,0:T(8,128)(2,1)S(1)}, bf16[4,208,128]{2,1,0:T(8,128)(2,1)S(1)}, u32[]{:S(2)}, u32[]{:S(2)}) collective-permute-start(bf16[4,208,128]{2,1,0:T(8,128)(2,1)S(1)} %shard_map.39.refs_0_), channel_id=1, source_target_pairs={{0,21},{1,20},{2,23},{3,22},{4,17},{5,16},{6,19},{7,18},{16,5},{17... | collective-permute-start | bytes 638984 | tf_op jit(solution)/shard_map/ppermute | solution.py:43
  35.9 0.2 collective-permute-start.3
  36.1 2.3 %collective-permute-start.2 = (bf16[4,208,128]{2,1,0:T(8,128)(2,1)S(1)}, bf16[4,208,128]{2,1,0:T(8,128)(2,1)S(1)}, u32[]{:S(2)}, u32[]{:S(2)}) collective-permute-start(bf16[4,208,128]{2,1,0:T(8,128)(2,1)S(1)} %shard_map.39.refs_0_), channel_id=1, source_target_pairs={{0,3},{1,2},{2,1},{3,0},{4,7},{5,6},{6,5},{7,4},{16,19},{17,18},{1... | collective-permute-start | bytes 638984 | tf_op jit(solution)/shard_map/ppermute | solution.py:43
  38.4 5.8 %collective-permute-done.6.refs_7_ = bf16[4,208,128]{2,1,0:T(8,128)(2,1)S(1)} collective-permute-done((bf16[4,208,128]{2,1,0:T(8,128)(2,1)S(1)}, bf16[4,208,128]{2,1,0:T(8,128)(2,1)S(1)}, u32[]{:S(2)}, u32[]{:S(2)}) %collective-permute-start.6) | collective-permute-done | bytes 213024 | tf_op jit(solution)/shard_map/ppermute | solution.py:43
  44.2 3.2 %collective-permute-done.4.refs_5_ = bf16[4,208,128]{2,1,0:T(8,128)(2,1)S(1)} collective-permute-done((bf16[4,208,128]{2,1,0:T(8,128)(2,1)S(1)}, bf16[4,208,128]{2,1,0:T(8,128)(2,1)S(1)}, u32[]{:S(2)}, u32[]{:S(2)}) %collective-permute-start.4) | collective-permute-done | bytes 213024 | tf_op jit(solution)/shard_map/ppermute | solution.py:43
  47.4 5.5 %collective-permute-done.3.refs_4_ = bf16[4,208,128]{2,1,0:T(8,128)(2,1)S(1)} collective-permute-done((bf16[4,208,128]{2,1,0:T(8,128)(2,1)S(1)}, bf16[4,208,128]{2,1,0:T(8,128)(2,1)S(1)}, u32[]{:S(2)}, u32[]{:S(2)}) %collective-permute-start.3) | collective-permute-done | bytes 213024 | tf_op jit(solution)/shard_map/ppermute | solution.py:43
  52.9 0.2 collective-permute-done.2.refs_3_
  53.2 0.2 collective-permute-done.1.refs_2_
  53.4 0.7 copy-done.3
  54.1 2.1 %collective-permute-done.refs_1_ = bf16[4,208,128]{2,1,0:T(8,128)(2,1)S(1)} collective-permute-done((bf16[4,208,128]{2,1,0:T(8,128)(2,1)S(1)}, bf16[4,208,128]{2,1,0:T(8,128)(2,1)S(1)}, u32[]{:S(2)}, u32[]{:S(2)}) %collective-permute-start) | collective-permute-done | bytes 213024 | tf_op jit(solution)/shard_map/ppermute | solution.py:43
  56.2 0.7 copy-done.5
  56.9 1.2 collective-permute-start.7
  58.1 0.9 copy-done.4
  59.0 0.9 copy-done.6
  60.0 0.7 fusion.valid_ref
  60.7 1.1 collective-permute-done.7.other_ref
  61.9 0.6 shard_map.41.values_ref
  62.5 17.8 %shard_map.42 = bf16[32,208,128]{2,1,0:T(8,128)(2,1)S(1)} custom-call(s32[32]{0:T(128)S(1)} %fusion.valid_ref, bf16[32,208,128]{2,1,0:T(8,128)(2,1)S(1)} %bitcast.11, bf16[16,512,128]{2,1,0:T(8,128)(2,1)S(1)} %all-to-all-done.1.own_ref, bf16[16,512,128]{2,1,0:T(8,128)(2,1)S(1)} %collective-permute-done.7.other_ref, ...), custom_call_target="tpu_custom_call" | custom-call | flops 20000000000 | bytes 8388608 | tf_op jit(solution)/shard_map/pallas_call | solution.py:295
  80.3 30.3 %all_to_all.20.part_ref = bf16[8,4,208,128]{3,2,1,0:T(8,128)(2,1)S(1)} all-to-all(bf16[8,4,208,128]{3,2,1,0:T(8,128)(2,1)S(1)} %bitcast.12), channel_id=1, replica_groups={{0,1,2,3,20,21,22,23},{16,17,18,19,4,5,6,7},{8,9,10,11,28,29,30,31},{24..., dimensions={0} | all-to-all | bytes 3407872 | tf_op jit(solution)/shard_map/all_to_all | solution.py:50
  110.5 1.0 shard_map.43
  111.6 18.4 %all_to_all.21 = bf16[16,192,128]{2,1,0:T(8,128)(2,1)} all-to-all(bf16[16,192,128]{2,1,0:T(8,128)(2,1)S(1)} %shard_map.43), channel_id=1, replica_groups=mesh['y'=4,'z_lo'=2,'core'=2,'col'=8] {'y','z_lo','core'}, dimensions={0} | all-to-all | bytes 1572864 | tf_op jit(solution)/shard_map/all_to_all | solution.py:393
  129.9 1.9 %shard_map.44 = bf16[256,1536]{1,0:T(8,128)(2,1)} custom-call(bf16[8,2,192,128]{3,2,1,0:T(8,128)(2,1)} %bitcast.16), custom_call_target="tpu_custom_call" | custom-call | bytes 1572864 | tf_op jit(solution)/shard_map/pallas_call | solution.py:358
  (15 shorter events, 0.1 us)
Async XLA Ops:
  0.0 9.5 %copy-start = (bf16[16,16,3,1536]{3,1,2,0:T(8,128)(2,1)S(1)}, bf16[16,16,3,1536]{3,1,2,0:T(8,128)(2,1)}, u32[]{:S(2)}) copy-start(bf16[16,16,3,1536]{3,1,2,0:T(8,128)(2,1)} %param.4) | copy-start | bytes 7077892
  0.0 9.5 %copy-start.7 = (s32[4,1]{0,1:T(1,128)S(1)}, s32[4,1]{0,1:T(1,128)}, u32[]{:S(2)}) copy-start(s32[4,1]{0,1:T(1,128)} %param.5) | copy-start | bytes 52
  2.1 20.0 %all-to-all-start = ((bf16[16,192,128]{2,1,0:T(8,128)(2,1)}), bf16[16,192,128]{2,1,0:T(8,128)(2,1)S(1)}, u32[]{:S(2)}, u32[]{:S(2)}) async-start(bf16[16,192,128]{2,1,0:T(8,128)(2,1)} %bitcast.17), calls=%async_computation | async-start | bytes 1572864 | tf_op jit(solution)/shard_map/all_to_all | solution.py:376
  9.5 1.4 %copy-start.2 = (bf16[16,16,2,1536]{3,2,1,0:T(2,128)(2,1)S(1)}, bf16[16,16,2,1536]{3,2,1,0:T(2,128)(2,1)}, u32[]{:S(2)}) copy-start(bf16[16,16,2,1536]{3,2,1,0:T(2,128)(2,1)} %cache_ref.1) | copy-start | bytes 4718596
  13.6 1.3 %copy-start.1 = (bf16[16,512,128]{2,1,0:T(8,128)(2,1)}, bf16[16,512,128]{2,1,0:T(8,128)(2,1)S(1)}, u32[]{:S(2)}) copy-start(bf16[16,512,128]{2,1,0:T(8,128)(2,1)S(1)} %shard_map.38) | copy-start | bytes 6291460
  22.7 34.2 %all-to-all-start.1 = ((bf16[16,512,128]{2,1,0:T(8,128)(2,1)}), bf16[16,512,128]{2,1,0:T(8,128)(2,1)S(1)}, u32[]{:S(2)}, u32[]{:S(2)}) async-start(bf16[16,512,128]{2,1,0:T(8,128)(2,1)} %copy-done.1), calls=%async_computation.1 | async-start | bytes 4194304 | tf_op jit(solution)/shard_map/all_to_all | solution.py:381
  27.3 16.9 %collective-permute-start.6 = (bf16[4,208,128]{2,1,0:T(8,128)(2,1)S(1)}, bf16[4,208,128]{2,1,0:T(8,128)(2,1)S(1)}, u32[]{:S(2)}, u32[]{:S(2)}) collective-permute-start(bf16[4,208,128]{2,1,0:T(8,128)(2,1)S(1)} %shard_map.39.refs_0_), channel_id=1, source_target_pairs={{0,23},{1,22},{2,21},{3,20},{4,19},{5,18},{6,17},{7,16},{16,7},{17... | collective-permute-start | bytes 638984 | tf_op jit(solution)/shard_map/ppermute | solution.py:43
  33.0 11.2 %collective-permute-start.5 = (bf16[4,208,128]{2,1,0:T(8,128)(2,1)S(1)}, bf16[4,208,128]{2,1,0:T(8,128)(2,1)S(1)}, u32[]{:S(2)}, u32[]{:S(2)}) collective-permute-start(bf16[4,208,128]{2,1,0:T(8,128)(2,1)S(1)} %shard_map.39.refs_0_), channel_id=1, source_target_pairs={{0,22},{1,23},{2,20},{3,21},{4,18},{5,19},{6,16},{7,17},{16,6},{17... | collective-permute-start | bytes 638984 | tf_op jit(solution)/shard_map/ppermute | solution.py:43
  33.4 14.1 %collective-permute-start.4 = (bf16[4,208,128]{2,1,0:T(8,128)(2,1)S(1)}, bf16[4,208,128]{2,1,0:T(8,128)(2,1)S(1)}, u32[]{:S(2)}, u32[]{:S(2)}) collective-permute-start(bf16[4,208,128]{2,1,0:T(8,128)(2,1)S(1)} %shard_map.39.refs_0_), channel_id=1, source_target_pairs={{0,21},{1,20},{2,23},{3,22},{4,17},{5,16},{6,19},{7,18},{16,5},{17... | collective-permute-start | bytes 638984 | tf_op jit(solution)/shard_map/ppermute | solution.py:43
  35.9 17.0 %collective-permute-start.3 = (bf16[4,208,128]{2,1,0:T(8,128)(2,1)S(1)}, bf16[4,208,128]{2,1,0:T(8,128)(2,1)S(1)}, u32[]{:S(2)}, u32[]{:S(2)}) collective-permute-start(bf16[4,208,128]{2,1,0:T(8,128)(2,1)S(1)} %shard_map.39.refs_0_), channel_id=1, source_target_pairs={{0,20},{1,21},{2,22},{3,23},{4,16},{5,17},{6,18},{7,19},{16,4},{17... | collective-permute-start | bytes 638984 | tf_op jit(solution)/shard_map/ppermute | solution.py:43
  36.1 17.1 %collective-permute-start.2 = (bf16[4,208,128]{2,1,0:T(8,128)(2,1)S(1)}, bf16[4,208,128]{2,1,0:T(8,128)(2,1)S(1)}, u32[]{:S(2)}, u32[]{:S(2)}) collective-permute-start(bf16[4,208,128]{2,1,0:T(8,128)(2,1)S(1)} %shard_map.39.refs_0_), channel_id=1, source_target_pairs={{0,3},{1,2},{2,1},{3,0},{4,7},{5,6},{6,5},{7,4},{16,19},{17,18},{1... | collective-permute-start | bytes 638984 | tf_op jit(solution)/shard_map/ppermute | solution.py:43
  44.2 9.2 %collective-permute-start.1 = (bf16[4,208,128]{2,1,0:T(8,128)(2,1)S(1)}, bf16[4,208,128]{2,1,0:T(8,128)(2,1)S(1)}, u32[]{:S(2)}, u32[]{:S(2)}) collective-permute-start(bf16[4,208,128]{2,1,0:T(8,128)(2,1)S(1)} %shard_map.39.refs_0_), channel_id=1, source_target_pairs={{0,2},{1,3},{2,0},{3,1},{4,6},{5,7},{6,4},{7,5},{16,18},{17,19},{1... | collective-permute-start | bytes 638984 | tf_op jit(solution)/shard_map/ppermute | solution.py:43
  44.2 12.0 %collective-permute-start = (bf16[4,208,128]{2,1,0:T(8,128)(2,1)S(1)}, bf16[4,208,128]{2,1,0:T(8,128)(2,1)S(1)}, u32[]{:S(2)}, u32[]{:S(2)}) collective-permute-start(bf16[4,208,128]{2,1,0:T(8,128)(2,1)S(1)} %shard_map.39.refs_0_), channel_id=1, source_target_pairs={{0,1},{1,0},{2,3},{3,2},{4,5},{5,4},{6,7},{7,6},{16,17},{17,16},{1... | collective-permute-start | bytes 638984 | tf_op jit(solution)/shard_map/ppermute | solution.py:43
  53.4 0.7 copy-start.3
  56.2 0.7 copy-start.5
  56.9 5.0 %collective-permute-start.7 = (bf16[16,512,128]{2,1,0:T(8,128)(2,1)S(1)}, bf16[16,512,128]{2,1,0:T(8,128)(2,1)S(1)}, u32[]{:S(2)}, u32[]{:S(2)}) collective-permute-start(bf16[16,512,128]{2,1,0:T(8,128)(2,1)S(1)} %all-to-all-done.1.own_ref), channel_id=1, source_target_pairs={{0,8},{8,0},{1,9},{9,1},{2,10},{10,2},{3,11},{11,3},{4,12},{12,4},... | collective-permute-start | bytes 6291464 | tf_op jit(solution)/shard_map/ppermute | solution.py:385
  58.1 0.9 copy-start.4
  59.0 0.9 copy-start.6

commit v7 on v6

--- a/solution.py
+++ b/solution.py
@@ -15,6 +15,7 @@
 KV_ROWS = 4 * HALF
 Q_ROWS = HALF + QUART
 SLOT_ROWS = Q_ROWS + 16
+FLAG_ROWS = 16
 GROUP = 8
 KEY_BLOCK = 512
 MIB = 1024 * 1024
@@ -157,13 +158,13 @@
 
 def pick_kernel(rows_ref, got_ref, out_ref):
     bands = got_ref.shape[0]
+    row_ids = lax.broadcasted_iota(jnp.int32, (FLAG_ROWS, DEPTH), 0)
+    flags = jnp.zeros((FLAG_ROWS, DEPTH), jnp.float32)
     for slot in range(SLOTS):
         row = rows_ref[slot]
-        rows = got_ref[jnp.minimum(row, bands - 1)]
-        flag = jnp.where(row < bands, 1.0, 0.0)
-        flags = jnp.full((SLOT_ROWS - Q_ROWS, DEPTH), flag, jnp.float32).astype(jnp.bfloat16)
-        out_ref[slot, 0:Q_ROWS, :] = rows
-        out_ref[slot, Q_ROWS:SLOT_ROWS, :] = flags
+        out_ref[slot * Q_ROWS : (slot + 1) * Q_ROWS, :] = got_ref[jnp.minimum(row, bands - 1)]
+        flags = jnp.where(row_ids == slot, jnp.where(row < bands, 1.0, 0.0), flags)
+    out_ref[SLOTS * Q_ROWS :, :] = flags.astype(jnp.bfloat16)
 
 
 def pick(listed_rows, received):
@@ -171,8 +172,8 @@
         pick_kernel,
         in_specs=[smem(), vmem()],
         out_specs=vmem(),
-        out_shape=jax.ShapeDtypeStruct((SLOTS, SLOT_ROWS, DEPTH), jnp.bfloat16),
-        cost_estimate=cost(0, 2 * 212992),
+        out_shape=jax.ShapeDtypeStruct((SLOTS * Q_ROWS + FLAG_ROWS, DEPTH), jnp.bfloat16),
+        cost_estimate=cost(0, 2 * 200704),
         compiler_params=pltpu.CompilerParams(vmem_limit_bytes=16 * MIB),
     )(listed_rows, received)
 
@@ -229,7 +230,7 @@
 
 
 def attend_kernel(valid_ref, q_ref, own_ref, other_ref, values_ref, out_ref, table):
-    slots = q_ref.shape[0]
+    slots = q_ref.shape[0] * SLOTS
 
     def note(slot, count):
         is_valid = valid_ref[slot]
@@ -248,9 +249,15 @@
 
     def attend_tiles(start, size):
         picks = [table[start + i] for i in range(size)]
-        full = jnp.concatenate([q_ref[pick, 0:HALF, :] for pick in picks], axis=0)
+        starts = [pl.multiple_of(pick % SLOTS * Q_ROWS, QUART) for pick in picks]
+        full = jnp.concatenate(
+            [q_ref[pick // SLOTS, pl.ds(at, HALF), :] for pick, at in zip(picks, starts)], axis=0
+        )
         out_full, lse_full = attend_rows(full, kv_refs, values_ref, 0)
-        shared = jnp.concatenate([q_ref[pick, HALF:Q_ROWS, :] for pick in picks], axis=0)
+        shared = jnp.concatenate(
+            [q_ref[pick // SLOTS, pl.ds(at + HALF, QUART), :] for pick, at in zip(picks, starts)],
+            axis=0,
+        )
         out_shared, lse_shared = attend_rows(shared, kv_refs, values_ref, 1)
         row_ids = lax.broadcasted_iota(jnp.int32, (16, DEPTH), 0)
         picks = [jnp.bitwise_xor(pick, SLOTS * lax.axis_index("col")) for pick in picks]
@@ -291,7 +298,7 @@
 
 
 def attend(valid, queries, own, other, values):
-    slots = queries.shape[0]
+    slots = queries.shape[0] * SLOTS
     return pl.pallas_call(
         attend_kernel,
         in_specs=[smem(), vmem(), vmem(), vmem(), vmem()],
@@ -383,8 +390,8 @@
     pieces, own = lax.optimization_barrier((pieces, own))
     queries = join(pieces)
     other = lax.ppermute(own, "core", [(0, 1), (1, 0)])
-    queries = queries.reshape(col_count * SLOTS, SLOT_ROWS, DEPTH)
-    valid = queries[:, Q_ROWS, 0].astype(jnp.int32)
+    flags = queries[:, SLOTS * Q_ROWS : SLOTS * Q_ROWS + SLOTS, 0]
+    valid = flags.reshape(col_count * SLOTS).astype(jnp.int32)
 
     partials = attend(valid, queries, own, other, widen(own, other))
     partials = partials.reshape(col_count, SLOTS, SLOT_ROWS, DEPTH)

time: 132 us -> 135 us (1.023)
  Pallas kernels: 26.9 us -> 32.3 us
    pallas_call x1, Pallas kernels: 17.8 us -> 21.3 us  [attend(): pl.pallas_call(attend_kernel, in_specs=[smem(), vmem(), vmem(), vmem(), v...]
    pallas_call x1, Pallas kernels: 0.62 us -> 2.21 us  [widen(): pl.pallas_call(widen_kernel, in_specs=[vmem(), vmem()], out_specs=vmem(),...]
  transfers between devices with their start and end apart: 10 -> 10, of which waited for: 8 -> 7; matrix products, arithmetic and copies ran while one was open for 1% -> 0% of each run, Pallas kernels for 2% -> 2%
where the time goes in v7:
time: 135 us; the launch traced here: 136 us
  blocking collectives  48.7 us (36%)
  Pallas kernels  32.3 us (24%)
  waiting for transfers between devices  25 us (19%)
  starting transfers between devices  24.2 us (18%)
  local copies, waits for them, and re-layouts  5.59 us (4%)
    all_to_all x1, blocking collectives, across(): lax.all_to_all(x, ('z_lo', 'col'), 0, 0, axis_index_groups=groups, tiled=...  30.5 us
    pallas_call x1, Pallas kernels, attend(): pl.pallas_call(attend_kernel, in_specs=[smem(), vmem(), vmem(), vmem(), v...  21.3 us
    all_to_all x1, blocking collectives, per_device(): finished = lax.all_to_all(finished, ROW, 0, 0, tiled=True)  18.2 us
    ppermute x7, waiting for transfers between devices, shift(): return lax.ppermute(x, ('z_lo', 'col'), pairs)  16.5 us
    ppermute x7, starting transfers between devices, shift(): return lax.ppermute(x, ('z_lo', 'col'), pairs)  11.1 us
    all_to_all x1, starting transfers between devices, per_device(): got_query = lax.all_to_all(query_message, ROW, 0, 0, tiled=True)  7.34 us
    all_to_all x1, waiting for transfers between devices, per_device(): got_query = lax.all_to_all(query_message, ROW, 0, 0, tiled=True)  7.15 us
    unnamed x16, local copies, waits for them, and re-layouts  5.51 us
  transfers between devices with their start and end apart: 10, of which 7 were waited for; matrix products, arithmetic and copies ran while one was open for 0% of the time, Pallas kernels for 2%

profile of v7, /device:TPU:1, one launch (start us, length us, event | category | flops | bytes accessed | tf_op | source)
XLA Modules:
  0.0 136.2 jit_solution(13995434520315635591)
XLA Ops:
  0.0 2.1 %shard_map.37 = bf16[8,2,192,128]{3,2,1,0:T(8,128)(2,1)} custom-call(bf16[16,3,16,1536]{3,2,1,0:T(8,128)(2,1)} %bitcast.6), custom_call_target="tpu_custom_call" | custom-call | bytes 1572864 | tf_op jit(solution)/shard_map/pallas_call | solution.py:73
  2.1 7.3 %all-to-all-start = ((bf16[16,192,128]{2,1,0:T(8,128)(2,1)}), bf16[16,192,128]{2,1,0:T(8,128)(2,1)S(1)}, u32[]{:S(2)}, u32[]{:S(2)}) async-start(bf16[16,192,128]{2,1,0:T(8,128)(2,1)} %bitcast.14), calls=%async_computation | async-start | bytes 1572864 | tf_op jit(solution)/shard_map/all_to_all | solution.py:383
  9.5 1.4 %copy-done.4 = bf16[16,16,2,1536]{3,2,1,0:T(2,128)(2,1)S(1)} copy-done((bf16[16,16,2,1536]{3,2,1,0:T(2,128)(2,1)S(1)}, bf16[16,16,2,1536]{3,2,1,0:T(2,128)(2,1)}, u32[]{:S(2)}) %copy-start.4) | copy-done | bytes 1572888
  10.9 2.7 %shard_map.38 = bf16[16,512,128]{2,1,0:T(8,128)(2,1)S(1)} custom-call(s32[4]{0:T(128)S(1)} %bitcast.10, bf16[16,16,2,1536]{3,2,1,0:T(2,128)(2,1)S(1)} %copy-done.4, bf16[16,3,16,1536]{3,2,1,0:T(8,128)(2,1)S(1)} %bitcast.7, bf16[16,3,16,1536]{3,2,1,0:T(8,128)(2,1)S(1)} %bitcast.8), custom_call_target="tpu_custom_call" | custom-call | bytes 5505024 | tf_op jit(solution)/shard_map/pallas_call | solution.py:126
  13.6 1.3 copy-done.1
  15.0 7.2 %all-to-all-done.got_ref = bf16[16,192,128]{2,1,0:T(8,128)(2,1)S(1)} async-done(((bf16[16,192,128]{2,1,0:T(8,128)(2,1)}), bf16[16,192,128]{2,1,0:T(8,128)(2,1)S(1)}, u32[]{:S(2)}, u32[]{:S(2)}) %all-to-all-start) | async-done | bytes 786464 | tf_op jit(solution)/shard_map/all_to_all | solution.py:383
  22.1 0.6 shard_map.39.refs_0_
  22.7 4.6 %all-to-all-start.1 = ((bf16[16,512,128]{2,1,0:T(8,128)(2,1)}), bf16[16,512,128]{2,1,0:T(8,128)(2,1)S(1)}, u32[]{:S(2)}, u32[]{:S(2)}) async-start(bf16[16,512,128]{2,1,0:T(8,128)(2,1)} %copy-done.1), calls=%async_computation.1 | async-start | bytes 4194304 | tf_op jit(solution)/shard_map/all_to_all | solution.py:388
  27.3 5.7 %collective-permute-start.6 = (bf16[784,128]{1,0:T(8,128)(2,1)S(1)}, bf16[784,128]{1,0:T(8,128)(2,1)S(1)}, u32[]{:S(2)}, u32[]{:S(2)}) collective-permute-start(bf16[784,128]{1,0:T(8,128)(2,1)S(1)} %shard_map.39.refs_0_), channel_id=1, source_target_pairs={{0,23},{1,22},{2,21},{3,20},{4,19},{5,18},{6,17},{7,16},{16,7},{17... | collective-permute-start | bytes 602120 | tf_op jit(solution)/shard_map/ppermute | solution.py:44
  33.0 0.4 collective-permute-start.5
  33.4 2.5 %collective-permute-start.4 = (bf16[784,128]{1,0:T(8,128)(2,1)S(1)}, bf16[784,128]{1,0:T(8,128)(2,1)S(1)}, u32[]{:S(2)}, u32[]{:S(2)}) collective-permute-start(bf16[784,128]{1,0:T(8,128)(2,1)S(1)} %shard_map.39.refs_0_), channel_id=1, source_target_pairs={{0,21},{1,20},{2,23},{3,22},{4,17},{5,16},{6,19},{7,18},{16,5},{17... | collective-permute-start | bytes 602120 | tf_op jit(solution)/shard_map/ppermute | solution.py:44
  35.9 0.2 collective-permute-start.3
  36.1 2.3 %collective-permute-start.2 = (bf16[784,128]{1,0:T(8,128)(2,1)S(1)}, bf16[784,128]{1,0:T(8,128)(2,1)S(1)}, u32[]{:S(2)}, u32[]{:S(2)}) collective-permute-start(bf16[784,128]{1,0:T(8,128)(2,1)S(1)} %shard_map.39.refs_0_), channel_id=1, source_target_pairs={{0,3},{1,2},{2,1},{3,0},{4,7},{5,6},{6,5},{7,4},{16,19},{17,18},{1... | collective-permute-start | bytes 602120 | tf_op jit(solution)/shard_map/ppermute | solution.py:44
  38.4 5.0 %collective-permute-done.6.refs_7_ = bf16[784,128]{1,0:T(8,128)(2,1)S(1)} collective-permute-done((bf16[784,128]{1,0:T(8,128)(2,1)S(1)}, bf16[784,128]{1,0:T(8,128)(2,1)S(1)}, u32[]{:S(2)}, u32[]{:S(2)}) %collective-permute-start.6) | collective-permute-done | bytes 200736 | tf_op jit(solution)/shard_map/ppermute | solution.py:44
  43.4 3.5 %collective-permute-done.4.refs_5_ = bf16[784,128]{1,0:T(8,128)(2,1)S(1)} collective-permute-done((bf16[784,128]{1,0:T(8,128)(2,1)S(1)}, bf16[784,128]{1,0:T(8,128)(2,1)S(1)}, u32[]{:S(2)}, u32[]{:S(2)}) %collective-permute-start.4) | collective-permute-done | bytes 200736 | tf_op jit(solution)/shard_map/ppermute | solution.py:44
  46.9 5.2 %collective-permute-done.3.refs_4_ = bf16[784,128]{1,0:T(8,128)(2,1)S(1)} collective-permute-done((bf16[784,128]{1,0:T(8,128)(2,1)S(1)}, bf16[784,128]{1,0:T(8,128)(2,1)S(1)}, u32[]{:S(2)}, u32[]{:S(2)}) %collective-permute-start.3) | collective-permute-done | bytes 200736 | tf_op jit(solution)/shard_map/ppermute | solution.py:44
  52.1 0.2 collective-permute-done.1.refs_2_
  52.4 2.5 %collective-permute-done.refs_1_ = bf16[784,128]{1,0:T(8,128)(2,1)S(1)} collective-permute-done((bf16[784,128]{1,0:T(8,128)(2,1)S(1)}, bf16[784,128]{1,0:T(8,128)(2,1)S(1)}, u32[]{:S(2)}, u32[]{:S(2)}) %collective-permute-start) | collective-permute-done | bytes 200736 | tf_op jit(solution)/shard_map/ppermute | solution.py:44
  54.9 0.7 copy-done.5
  55.5 1.2 collective-permute-start.7
  56.7 0.9 copy-done.6
  57.7 0.1 shard_map.40.q_ref
  57.8 0.2 convert_reduce_fusion
  58.0 1.1 copy-done.2
  59.1 0.1 reshape.18.valid_ref
  59.2 1.4 %collective-permute-done.7.other_ref = bf16[16,512,128]{2,1,0:T(8,128)(2,1)} collective-permute-done((bf16[16,512,128]{2,1,0:T(8,128)(2,1)S(1)}, bf16[16,512,128]{2,1,0:T(8,128)(2,1)}, u32[]{:S(2)}, u32[]{:S(2)}) %collective-permute-start.7) | collective-permute-done | bytes 2097184 | tf_op jit(solution)/shard_map/ppermute | solution.py:392
  60.6 2.2 %shard_map.41.values_ref = bf16[2,4096,256]{2,1,0:T(8,128)(2,1)S(1)} custom-call(bf16[16,512,128]{2,1,0:T(8,128)(2,1)S(1)} %all-to-all-done.1.own_ref, bf16[16,512,128]{2,1,0:T(8,128)(2,1)} %collective-permute-done.7.other_ref), custom_call_target="tpu_custom_call" | custom-call | bytes 8388608 | tf_op jit(solution)/shard_map/pallas_call | solution.py:191
  62.9 21.3 %shard_map.42 = bf16[32,208,128]{2,1,0:T(8,128)(2,1)S(1)} custom-call(s32[32]{0:T(128)S(1)} %reshape.18.valid_ref, bf16[8,784,128]{2,1,0:T(8,128)(2,1)S(1)} %copy-done.3, bf16[16,512,128]{2,1,0:T(8,128)(2,1)S(1)} %all-to-all-done.1.own_ref, bf16[16,512,128]{2,1,0:T(8,128)(2,1)} %collective-permute-done.7.other_ref, ...), custom_call_target="tpu_custom_call" | custom-call | flops 20000000000 | bytes 8388608 | tf_op jit(solution)/shard_map/pallas_call | solution.py:302
  84.2 30.5 %all_to_all.20.part_ref = bf16[8,4,208,128]{3,2,1,0:T(8,128)(2,1)S(1)} all-to-all(bf16[8,4,208,128]{3,2,1,0:T(8,128)(2,1)S(1)} %bitcast.9), channel_id=1, replica_groups={{0,1,2,3,20,21,22,23},{16,17,18,19,4,5,6,7},{8,9,10,11,28,29,30,31},{24..., dimensions={0} | all-to-all | bytes 3407872 | tf_op jit(solution)/shard_map/all_to_all | solution.py:51
  114.7 1.4 %shard_map.43 = bf16[16,192,128]{2,1,0:T(8,128)(2,1)S(1)} custom-call(s32[4]{0:T(128)S(1)} %bitcast.12, bf16[8,4,208,128]{3,2,1,0:T(8,128)(2,1)S(1)} %all_to_all.20.part_ref), custom_call_target="tpu_custom_call" | custom-call | tf_op jit(solution)/shard_map/pallas_call | solution.py:344
  116.0 18.2 %all_to_all.21 = bf16[16,192,128]{2,1,0:T(8,128)(2,1)} all-to-all(bf16[16,192,128]{2,1,0:T(8,128)(2,1)S(1)} %shard_map.43), channel_id=1, replica_groups=mesh['y'=4,'z_lo'=2,'core'=2,'col'=8] {'y','z_lo','core'}, dimensions={0} | all-to-all | bytes 1572864 | tf_op jit(solution)/shard_map/all_to_all | solution.py:400
  134.3 1.9 %shard_map.44 = bf16[256,1536]{1,0:T(8,128)(2,1)} custom-call(bf16[8,2,192,128]{3,2,1,0:T(8,128)(2,1)} %bitcast.13), custom_call_target="tpu_custom_call" | custom-call | bytes 1572864 | tf_op jit(solution)/shard_map/pallas_call | solution.py:365
  (16 shorter events, 0.0 us)
Async XLA Ops:
  0.0 9.5 %copy-start = (bf16[16,16,3,1536]{3,1,2,0:T(8,128)(2,1)S(1)}, bf16[16,16,3,1536]{3,1,2,0:T(8,128)(2,1)}, u32[]{:S(2)}) copy-start(bf16[16,16,3,1536]{3,1,2,0:T(8,128)(2,1)} %param.4) | copy-start | bytes 7077892
  0.0 9.5 %copy-start.7 = (s32[4,1]{0,1:T(1,128)S(1)}, s32[4,1]{0,1:T(1,128)}, u32[]{:S(2)}) copy-start(s32[4,1]{0,1:T(1,128)} %param.5) | copy-start | bytes 52
  2.1 20.0 %all-to-all-start = ((bf16[16,192,128]{2,1,0:T(8,128)(2,1)}), bf16[16,192,128]{2,1,0:T(8,128)(2,1)S(1)}, u32[]{:S(2)}, u32[]{:S(2)}) async-start(bf16[16,192,128]{2,1,0:T(8,128)(2,1)} %bitcast.14), calls=%async_computation | async-start | bytes 1572864 | tf_op jit(solution)/shard_map/all_to_all | solution.py:383
  9.5 1.4 %copy-start.4 = (bf16[16,16,2,1536]{3,2,1,0:T(2,128)(2,1)S(1)}, bf16[16,16,2,1536]{3,2,1,0:T(2,128)(2,1)}, u32[]{:S(2)}) copy-start(bf16[16,16,2,1536]{3,2,1,0:T(2,128)(2,1)} %cache_ref.1) | copy-start | bytes 4718596
  13.6 1.3 copy-start.1
  22.7 32.9 %all-to-all-start.1 = ((bf16[16,512,128]{2,1,0:T(8,128)(2,1)}), bf16[16,512,128]{2,1,0:T(8,128)(2,1)S(1)}, u32[]{:S(2)}, u32[]{:S(2)}) async-start(bf16[16,512,128]{2,1,0:T(8,128)(2,1)} %copy-done.1), calls=%async_computation.1 | async-start | bytes 4194304 | tf_op jit(solution)/shard_map/all_to_all | solution.py:388
  27.3 16.1 %collective-permute-start.6 = (bf16[784,128]{1,0:T(8,128)(2,1)S(1)}, bf16[784,128]{1,0:T(8,128)(2,1)S(1)}, u32[]{:S(2)}, u32[]{:S(2)}) collective-permute-start(bf16[784,128]{1,0:T(8,128)(2,1)S(1)} %shard_map.39.refs_0_), channel_id=1, source_target_pairs={{0,23},{1,22},{2,21},{3,20},{4,19},{5,18},{6,17},{7,16},{16,7},{17... | collective-permute-start | bytes 602120 | tf_op jit(solution)/shard_map/ppermute | solution.py:44
  33.0 10.4 %collective-permute-start.5 = (bf16[784,128]{1,0:T(8,128)(2,1)S(1)}, bf16[784,128]{1,0:T(8,128)(2,1)S(1)}, u32[]{:S(2)}, u32[]{:S(2)}) collective-permute-start(bf16[784,128]{1,0:T(8,128)(2,1)S(1)} %shard_map.39.refs_0_), channel_id=1, source_target_pairs={{0,22},{1,23},{2,20},{3,21},{4,18},{5,19},{6,16},{7,17},{16,6},{17... | collective-permute-start | bytes 602120 | tf_op jit(solution)/shard_map/ppermute | solution.py:44
  33.4 13.5 %collective-permute-start.4 = (bf16[784,128]{1,0:T(8,128)(2,1)S(1)}, bf16[784,128]{1,0:T(8,128)(2,1)S(1)}, u32[]{:S(2)}, u32[]{:S(2)}) collective-permute-start(bf16[784,128]{1,0:T(8,128)(2,1)S(1)} %shard_map.39.refs_0_), channel_id=1, source_target_pairs={{0,21},{1,20},{2,23},{3,22},{4,17},{5,16},{6,19},{7,18},{16,5},{17... | collective-permute-start | bytes 602120 | tf_op jit(solution)/shard_map/ppermute | solution.py:44
  35.9 16.2 %collective-permute-start.3 = (bf16[784,128]{1,0:T(8,128)(2,1)S(1)}, bf16[784,128]{1,0:T(8,128)(2,1)S(1)}, u32[]{:S(2)}, u32[]{:S(2)}) collective-permute-start(bf16[784,128]{1,0:T(8,128)(2,1)S(1)} %shard_map.39.refs_0_), channel_id=1, source_target_pairs={{0,20},{1,21},{2,22},{3,23},{4,16},{5,17},{6,18},{7,19},{16,4},{17... | collective-permute-start | bytes 602120 | tf_op jit(solution)/shard_map/ppermute | solution.py:44
  36.1 16.1 %collective-permute-start.2 = (bf16[784,128]{1,0:T(8,128)(2,1)S(1)}, bf16[784,128]{1,0:T(8,128)(2,1)S(1)}, u32[]{:S(2)}, u32[]{:S(2)}) collective-permute-start(bf16[784,128]{1,0:T(8,128)(2,1)S(1)} %shard_map.39.refs_0_), channel_id=1, source_target_pairs={{0,3},{1,2},{2,1},{3,0},{4,7},{5,6},{6,5},{7,4},{16,19},{17,18},{1... | collective-permute-start | bytes 602120 | tf_op jit(solution)/shard_map/ppermute | solution.py:44
  43.4 9.0 %collective-permute-start.1 = (bf16[784,128]{1,0:T(8,128)(2,1)S(1)}, bf16[784,128]{1,0:T(8,128)(2,1)S(1)}, u32[]{:S(2)}, u32[]{:S(2)}) collective-permute-start(bf16[784,128]{1,0:T(8,128)(2,1)S(1)} %shard_map.39.refs_0_), channel_id=1, source_target_pairs={{0,2},{1,3},{2,0},{3,1},{4,6},{5,7},{6,4},{7,5},{16,18},{17,19},{1... | collective-permute-start | bytes 602120 | tf_op jit(solution)/shard_map/ppermute | solution.py:44
  43.4 11.4 %collective-permute-start = (bf16[784,128]{1,0:T(8,128)(2,1)S(1)}, bf16[784,128]{1,0:T(8,128)(2,1)S(1)}, u32[]{:S(2)}, u32[]{:S(2)}) collective-permute-start(bf16[784,128]{1,0:T(8,128)(2,1)S(1)} %shard_map.39.refs_0_), channel_id=1, source_target_pairs={{0,1},{1,0},{2,3},{3,2},{4,5},{5,4},{6,7},{7,6},{16,17},{17,16},{1... | collective-permute-start | bytes 602120 | tf_op jit(solution)/shard_map/ppermute | solution.py:44
  54.9 0.7 copy-start.5
  55.5 5.1 %collective-permute-start.7 = (bf16[16,512,128]{2,1,0:T(8,128)(2,1)S(1)}, bf16[16,512,128]{2,1,0:T(8,128)(2,1)}, u32[]{:S(2)}, u32[]{:S(2)}) collective-permute-start(bf16[16,512,128]{2,1,0:T(8,128)(2,1)S(1)} %all-to-all-done.1.own_ref), channel_id=1, source_target_pairs={{0,8},{8,0},{1,9},{9,1},{2,10},{10,2},{3,11},{11,3},{4,12},{12,4},... | collective-permute-start | bytes 6291464 | tf_op jit(solution)/shard_map/ppermute | solution.py:392
  56.7 0.9 copy-start.6
  58.0 1.2 copy-start.2
  59.2 3.6 %copy-start.3 = (bf16[8,784,128]{2,1,0:T(8,128)(2,1)S(1)}, bf16[8,784,128]{2,1,0:T(8,128)(2,1)}, u32[]{:S(2)}) copy-start(bf16[8,784,128]{2,1,0:T(8,128)(2,1)} %copy-done.2) | copy-start | bytes 4816900
